TPU v7x, 32 devices: a whole 2x2x4 slice. The times are simulated.
32 devices in a mesh: hist: 4 (over z), cand: 8 (over y, x, core).
Axes of the slice: x: 2, y: 2, z: 4, core: 2. Of those that a mesh axis runs over, the one named last changes fastest.
Arguments:
- candidates: bfloat16 [8, 256, 1024], P('cand'), may hold values from -6 to 6
- input_gain: float32 [1024], replicated, may hold values from 0.1 to 1.9
- proj_weight: bfloat16 [2, 1024, 1024], P(None, None, 'hist'), may hold values from -0.1875 to 0.1875
- history_cache: bfloat16 [320, 8, 512, 256], P('cand', 'hist'), may hold values from -6 to 6
- slot_user: int32 [320], P('cand'), may hold values from 0 to 7
- slot_block: int32 [320], P('cand'), may hold values from -1 to 31, as said below
- history_len: int32 [8], replicated, may hold values from 1537 to 16384
- attention_gain: float32 [1024], replicated, may hold values from 0.1 to 1.9
- out_weight: bfloat16 [1024, 1024], P(None, 'hist'), may hold values from -0.1875 to 0.1875
Outputs:
- result: bfloat16 [8, 256, 1024], P('cand', None, 'hist')
Inputs may be any that keep to these rules, and one draw needn't show every extreme that they name: Each pair of a user u and a block number b < ceil(history_len[u] / 512) is held by exactly one slot; every other slot has slot_block -1.
All inputs are finite; a program needn't handle non-finite values.
Results may differ from a plain program's by a relative error of at most 0.015.
Values may be sent and summed in bfloat16 or wider, within the bound.
No kernel may reach another device: no remote copies, remote signals or barrier semaphores. Data moves between devices by JAX's collectives and lax.ppermute only.
A program may use at most 128 MiB of HBM per device.

v0:
```python
import jax
import jax.numpy as jnp
from jax import lax
from jax.sharding import PartitionSpec as P

D = 1024
DH = 128


def layer_norm(rows, gain):
    row_mean = jnp.mean(rows, axis=-1, keepdims=True)
    centred = rows - row_mean
    row_var = jnp.mean(centred * centred, axis=-1, keepdims=True)
    return centred * lax.rsqrt(row_var + 1e-05) * gain


def local(
    candidates,
    input_gain,
    proj_weight,
    history_cache,
    slot_user,
    slot_block,
    history_len,
    attention_gain,
    out_weight,
):
    user_count = lax.axis_size("cand")
    cand_count = candidates.shape[1]
    head_cols = proj_weight.shape[2]
    heads_here = head_cols // DH
    slot_count = history_cache.shape[0]
    block_len = history_cache.shape[2]
    cand_rows = candidates.astype(jnp.float32)
    normed_input = layer_norm(cand_rows, input_gain).astype(jnp.bfloat16)
    flat_rows = normed_input.reshape(cand_count, D)
    gate_own = jax.nn.silu(
        jnp.dot(flat_rows, proj_weight[0], preferred_element_type=jnp.float32)
    ).astype(jnp.bfloat16)
    features = lax.all_gather(normed_input, "cand", axis=0, tiled=True)
    query_all = jax.nn.silu(
        jnp.dot(
            features.reshape(user_count * cand_count, D),
            proj_weight[1],
            preferred_element_type=jnp.float32,
        )
    )
    query_all = query_all.astype(jnp.bfloat16).reshape(user_count, cand_count, head_cols)
    slot_queries = jnp.take(query_all, slot_user, axis=0).reshape(
        slot_count, cand_count, heads_here, DH
    )
    cache_keys = history_cache[..., :DH]
    cache_values = history_cache[..., DH:]
    scores = jnp.einsum(
        "schd,shtd->shct", slot_queries, cache_keys, preferred_element_type=jnp.float32
    ) * DH ** (-0.5)
    user_ids = jnp.arange(user_count, dtype=jnp.int32)
    owner_hit = slot_user[:, None] == user_ids[None, :]
    lengths = jnp.sum(jnp.where(owner_hit, history_len[None, :], 0), axis=1)
    event_index = slot_block[:, None] * block_len + jnp.arange(block_len, dtype=jnp.int32)[None, :]
    live_mask = (slot_block[:, None] >= 0) & (event_index < lengths[:, None])
    weights = (jax.nn.silu(scores) * live_mask[:, None, None, :].astype(jnp.float32)).astype(
        jnp.bfloat16
    )
    partial_value = jnp.einsum(
        "shct,shtd->schd", weights, cache_values, preferred_element_type=jnp.float32
    )
    partial_value = partial_value.reshape(slot_count, cand_count, head_cols)
    owner_table = owner_hit.astype(jnp.float32)
    buffer = jnp.einsum("su,scw->ucw", owner_table, partial_value, precision=lax.Precision.HIGHEST)
    attn_head = lax.psum_scatter(
        buffer.astype(jnp.bfloat16), "cand", scatter_dimension=0, tiled=True
    ).astype(jnp.float32)
    first_col = lax.axis_index("hist") * head_cols
    attn_all, gate_all = (
        lax.all_gather(attn_head, "hist", axis=2, tiled=True),
        lax.all_gather(
            gate_own.astype(jnp.float32).reshape(1, cand_count, head_cols),
            "hist",
            axis=2,
            tiled=True,
        ),
    )
    gated = (layer_norm(attn_all, attention_gain) * gate_all).astype(jnp.bfloat16)
    cand_cols = lax.dynamic_slice_in_dim(cand_rows, first_col, head_cols, 2)
    projected = jnp.dot(
        gated.reshape(cand_count, D), out_weight, preferred_element_type=jnp.float32
    )
    result = cand_cols + projected.reshape(1, cand_count, head_cols)
    return result.astype(jnp.bfloat16)


def solution(mesh):
    return jax.shard_map(
        local,
        mesh=mesh,
        in_specs=(
            P("cand", None, None),
            P(),
            P(None, None, "hist"),
            P("cand", "hist", None, None),
            P("cand"),
            P("cand"),
            P(),
            P(),
            P(None, "hist"),
        ),
        out_specs=P("cand", None, "hist"),
        check_vma=False,
    )
```

profile of v0, /device:TPU:0, one launch (start us, length us, event | category | flops | bytes accessed | tf_op | source)
XLA Modules:
  0.0 216.0 jit_solution(8166014425885951037)
XLA Ops:
  6.5 0.0 copy-start
  6.5 0.0 all-gather.5.cloned.1.call-start
  6.5 1.2 convert_reduce_fusion
  7.8 1.3 multiply_reduce_fusion.1
  9.1 2.1 multiply_convert_fusion.3
  11.3 0.0 all-gather.5.cloned.1.call-update
  11.3 0.0 reduce-scatter.2.cloned.1.call-start
  11.3 0.7 compare_select_fusion
  12.0 0.8 select_reduce_fusion
  12.8 0.7 broadcast_compare_fusion
  13.4 0.7 broadcast_multiply_fusion.2
  14.1 0.7 compare_and_fusion
  14.7 0.1 fusion.39
  14.8 36.1 %all-gather.5.cloned.1.call-done = bf16[8,256,1024]{2,1,0:T(8,128)(2,1)} async-done(((bf16[1,256,1024]{2,1,0:T(8,128)(2,1)}), bf16[8,256,1024]{2,1,0:T(8,128)(2,1)}) %all-gather.5.cloned.1.call-update) | async-done | bytes 4194320 | tf_op jit(solution)/shard_map/all_gather | solution.py:40
  50.9 3.7 %multiply_convert_fusion.2 = bf16[2048,256]{1,0:T(8,128)(2,1)S(1)} fusion(bf16[2048,1024]{1,0:T(8,128)(2,1)} %bitcast.50, bf16[2,1024,256]{2,1,0:T(8,128)(2,1)} %param.11), kind=kOutput, calls=%fused_computation.9 | convolution fusion | flops 1076363264 | bytes 5767168 | tf_op jit(solution)/shard_map/dot_general | solution.py:42
  54.6 4.6 %gather_fusion = bf16[40,256,256]{2,1,0:T(8,128)(2,1)} fusion(bf16[8,256,256]{2,1,0:T(8,128)(2,1)S(1)} %bitcast.47, s32[1024]{0:T(1024)S(1)} %pad_clamp_fusion), kind=kCustom, calls=%fused_computation | custom fusion | bytes 10485920 | tf_op jit(solution)/shard_map/jit(_take)/gather | solution.py:49
  59.2 7.9 %copy.19 = bf16[40,256,256]{1,2,0:T(8,128)(2,1)} copy(bf16[40,256,256]{2,1,0:T(8,128)(2,1)} %gather_fusion) | data formatting | bytes 10485760 | tf_op jit(solution)/shard_map/jit(_take)/gather | solution.py:49
  67.1 24.6 %fusion = f32[40,2,256,128]{2,3,1,0:T(8,128)} fusion(f32[40,512]{1,0:T(8,128)S(1)} %fusion.39, bf16[40,2,512,256]{3,2,1,0:T(8,128)(2,1)} %param.12, bf16[40,256,2,128]{1,3,2,0:T(8,128)(2,1)} %bitcast.49, pred[40]{0:T(512)(128)(4,1)S(1)} %compare_and_fusion), kind=kOutput, calls=%fused_computation.2 | convolution fusion | flops 5444730880 | bytes 36782120 | tf_op jit(solution)/shard_map/shct,shtd->schd/dot_general | solution.py:65
  91.7 0.0 copy-start.4
  91.7 11.6 %copy.22 = f32[40,256,256]{2,0,1:T(8,128)} copy(f32[40,256,256]{1,2,0:T(8,128)} %bitcast.48) | data formatting | bytes 20971520 | tf_op jit(solution)/shard_map/reshape | solution.py:68
  103.3 0.0 copy-done.4
  103.3 0.0 copy-start.2
  103.3 0.0 copy-start.5
  103.3 0.0 copy-start.1
  103.3 0.0 copy-start.3
  103.3 7.6 %convolution_convert_fusion = bf16[8,256,256]{2,0,1:T(8,128)(2,1)S(1)} fusion(f32[40,256,256]{2,0,1:T(8,128)} %copy.22, s32[40]{0:T(128)S(1)} %copy-done.4), kind=kOutput, calls=%fused_computation.10 | convolution fusion | flops 252182848 | bytes 11534496 | tf_op jit(solution)/shard_map/su,scw->ucw/dot_general | solution.py:70
  110.9 1.2 copy.23
  112.1 0.0 reduce-scatter.2.cloned.1.call-update
  112.1 0.0 all-gather.7.cloned.1.call-start
  112.1 36.1 %reduce-scatter.2.cloned.1.call-done = bf16[1,256,256]{2,1,0:T(8,128)(2,1)} async-done(((bf16[8,256,256]{2,1,0:T(8,128)(2,1)}), bf16[1,256,256]{2,1,0:T(8,128)(2,1)}) %reduce-scatter.2.cloned.1.call-update) | async-done | bytes 131088 | tf_op jit(solution)/shard_map/reduce_scatter | solution.py:71
  148.3 1.7 convert_element_type.43
  149.9 0.0 all-gather.7.cloned.1.call-update
  150.0 0.0 all-gather.9.cloned.1.call-start
  150.0 0.0 copy-done.2
  150.0 0.0 copy-done.5
  150.0 1.0 fusion.33
  151.1 0.0 all-gather.9.cloned.1.call-update
  151.1 0.0 copy-done.1
  151.1 0.1 convert_element_type.37
  151.2 26.8 %all-gather.7.cloned.1.call-done = f32[1,256,1024]{2,1,0:T(8,128)} async-done(((f32[1,256,256]{2,1,0:T(8,128)}), f32[1,256,1024]{2,1,0:T(8,128)}) %all-gather.7.cloned.1.call-update) | async-done | bytes 1048592 | tf_op jit(solution)/shard_map/all_gather | solution.py:76
  178.0 1.4 reduce_sum.48
  179.4 1.5 multiply_reduce_fusion
  180.9 26.0 %all-gather.9.cloned.1.call-done = f32[256,1024]{1,0:T(8,128)} async-done(((f32[256,256]{1,0:T(8,128)}), f32[256,1024]{1,0:T(8,128)}) %all-gather.9.cloned.1.call-update) | async-done | bytes 1048592 | tf_op jit(solution)/shard_map/all_gather | solution.py:77
  206.9 0.0 copy-done
  206.9 0.0 copy-done.3
  206.9 2.6 %fusion.13 = bf16[1,256,256]{2,1,0:T(8,128)(2,1)} fusion(bf16[1024,256]{1,0:T(8,128)(2,1)S(1)} %copy-done, f32[256,1024]{1,0:T(8,128)} %all-gather.9.cloned.1.call-done, f32[1,256,1024]{2,1,0:T(8,128)} %all-gather.7.cloned.1.call-done, f32[1024]{0:T(1024)S(1)} %copy-done.3, f32[256]{0:T(256)S(1)} %add_rsqrt_fusion, f32[256]{0:T(256)S(1)} %broadcast_multiply_fusion, ...), kind=kOutput, calls=%fused_computation.13 | convolution fusion | flops 135659520 | bytes 3020804 | tf_op jit(solution)/shard_map/dot_general | solution.py:86
  (5 shorter events, 0.0 us)
Async XLA Ops:
  6.5 200.4 %copy-start = (bf16[1024,256]{1,0:T(8,128)(2,1)S(1)}, bf16[1024,256]{1,0:T(8,128)(2,1)}, u32[]{:S(2)}) copy-start(bf16[1024,256]{1,0:T(8,128)(2,1)} %param.17) | copy-start | bytes 1572868
  6.5 44.4 %all-gather.5.cloned.1.call-start = ((), (), s32[]{:S(2)}) async-start(), calls=%async_computation.1 | async-start | bytes 4718592 | tf_op jit(solution)/shard_map/all_gather | solution.py:40
  11.3 137.0 %reduce-scatter.2.cloned.1.call-start = ((), (), s32[]{:S(2)}) async-start(), calls=%async_computation.2 | async-start | bytes 1179648 | tf_op jit(solution)/shard_map/reduce_scatter | solution.py:71
  91.7 11.6 %copy-start.4 = (s32[40]{0:T(128)S(1)}, s32[40]{0:T(128)}, u32[]{:S(2)}) copy-start(s32[40]{0:T(128)} %param.13) | copy-start | bytes 484
  103.3 46.7 %copy-start.2 = (bf16[1,256,1024]{2,1,0:T(8,128)(2,1)S(1)}, bf16[1,256,1024]{2,1,0:T(8,128)(2,1)}, u32[]{:S(2)}) copy-start(bf16[1,256,1024]{2,1,0:T(8,128)(2,1)} %multiply_convert_fusion.3) | copy-start | bytes 1572868
  103.3 46.8 %copy-start.5 = (bf16[2,1024,256]{2,1,0:T(8,128)(2,1)S(1)}, bf16[2,1024,256]{2,1,0:T(8,128)(2,1)}, u32[]{:S(2)}) copy-start(bf16[2,1024,256]{2,1,0:T(8,128)(2,1)} %param.11) | copy-start | bytes 3145732
  103.3 47.8 %copy-start.1 = (bf16[1,256,1024]{2,1,0:T(8,128)(2,1)S(1)}, bf16[1,256,1024]{2,1,0:T(8,128)(2,1)}, u32[]{:S(2)}) copy-start(bf16[1,256,1024]{2,1,0:T(8,128)(2,1)} %param.9) | copy-start | bytes 1572868
  103.3 103.6 %copy-start.3 = (f32[1024]{0:T(1024)S(1)}, f32[1024]{0:T(1024)}, u32[]{:S(2)}) copy-start(f32[1024]{0:T(1024)} %param.16) | copy-start | bytes 12292
  112.1 65.9 %all-gather.7.cloned.1.call-start = ((), (), s32[]{:S(2)}) async-start(), calls=%async_computation.3 | async-start | bytes 1310720 | tf_op jit(solution)/shard_map/all_gather | solution.py:76
  150.0 57.0 %all-gather.9.cloned.1.call-start = ((), (), s32[]{:S(2)}) async-start(), calls=%async_computation.4 | async-start | bytes 1310720 | tf_op jit(solution)/shard_map/all_gather | solution.py:77
Sparse Core Ops, SparseCore 0:
  11.4 39.4 all-gather.4
  112.2 36.0 reduce-scatter.1
  150.1 27.9 all-gather.6
  179.5 27.4 all-gather.8
where the time goes:
time: 217 us; the launch traced here: 216 us
  waiting for transfers between devices  125 us (58%)
  matrix products  39.4 us (18%)
  local copies, waits for them, and re-layouts  25.3 us (12%)
  between operations  13.2 us (6%)
  other arithmetic  12.8 us (6%)
    reduce_scatter x1, waiting for transfers between devices, local(): lax.psum_scatter(buffer.astype(jnp.bfloat16), 'cand', scatter_dimension=0...  36.1 us
    all_gather x1, waiting for transfers between devices, local(): features = lax.all_gather(normed_input, 'cand', axis=0, tiled=True)  36.1 us
    all_gather x1, waiting for transfers between devices, local(): lax.all_gather(attn_head, 'hist', axis=2, tiled=True)  26.8 us
    all_gather x1, waiting for transfers between devices, local(): lax.all_gather(gate_own.astype(jnp.float32).reshape(1, cand_count, head_c...  26 us
    dot_general x1, matrix products, local(): jnp.einsum('shct,shtd->schd', weights, cache_values, preferred_element_ty...  24.6 us
    gather x2, local copies, waits for them, and re-layouts, local(): jnp.take(query_all, slot_user, axis=0)  12.5 us
    reshape x1, local copies, waits for them, and re-layouts, local(): partial_value = partial_value.reshape(slot_count, cand_count, head_cols)  11.6 us
    dot_general x1, matrix products, local(): jnp.einsum('su,scw->ucw', owner_table, partial_value, precision=lax.Preci...  7.58 us
  transfers between devices with their start and end apart: 4, of which 4 were waited for; matrix products, arithmetic and copies ran while one was open for 3% of the time, Pallas kernels for 0%

commit v1 on v0

v1 whole, which is shorter than its diff:
```python
import functools

import jax
import jax.numpy as jnp
from jax import lax
from jax.experimental import pallas as pl
from jax.experimental.pallas import tpu as pltpu
from jax.sharding import PartitionSpec as P

D = 1024
DH = 128
EPS = 1e-05
UNIT = 2
BUFS = 6
F32 = jnp.float32
BF16 = jnp.bfloat16
VMEM_BYTES = 32 * 1024 * 1024
HALF_SCALE = 0.5 * DH ** (-0.5)

VM = pl.BlockSpec(memory_space=pltpu.VMEM)
SM = pl.BlockSpec(memory_space=pltpu.SMEM)
HB = pl.BlockSpec(memory_space=pltpu.HBM)
ANY = pl.BlockSpec(memory_space=pl.ANY)


def params():
    return pltpu.CompilerParams(vmem_limit_bytes=VMEM_BYTES)


def silu_of_half(half):
    return half * jnp.tanh(half) + half


SLOT, OFFSET, LIVE, COUNT = range(4)


def project_kernel(
    block_len, cand_hbm, gain_hbm, weight_hbm, user_hbm, block_hbm, len_hbm, *refs
):
    heads = len(refs) - 10
    queries, gate_ref, plan = refs[:heads], refs[heads], refs[heads + 1]
    cand, gain, weight, user, block, length, sems = refs[heads + 2 : heads + 9]
    wsems = refs[heads + 9]
    ints = [
        pltpu.make_async_copy(src, dst, sems.at[i])
        for i, (src, dst) in enumerate([(user_hbm, user), (block_hbm, block), (len_hbm, length)])
    ]
    rows_in = [
        pltpu.make_async_copy(src, dst, sems.at[3 + i])
        for i, (src, dst) in enumerate([(cand_hbm, cand), (gain_hbm, gain)])
    ]
    weights_in = [
        pltpu.make_async_copy(weight_hbm.at[i], weight.at[i], wsems.at[i]) for i in range(2)
    ]
    for copy in ints + rows_in + weights_in[::-1]:
        copy.start()
    me = lax.axis_index("cand")
    slots = user.shape[0]
    for copy in ints:
        copy.wait()

    def note(parity, s, count):
        owner = user[s]
        number = block[s]
        offset = owner ^ me
        plan[SLOT, count] = s
        plan[OFFSET, count] = offset
        plan[LIVE, count] = length[owner] - number * block_len
        return count + ((number >= 0) & (offset % 2 == parity)).astype(jnp.int32)

    odd = lax.fori_loop(0, slots, functools.partial(note, 1), jnp.int32(0))
    count = lax.fori_loop(0, slots, functools.partial(note, 0), odd)
    for i in range(UNIT):
        plan[SLOT, count + i] = 0
        plan[OFFSET, count + i] = 0
        plan[LIVE, count + i] = 0
    plan[COUNT, 0] = odd
    plan[COUNT, 1] = count

    for copy in rows_in:
        copy.wait()
    rows = cand[0].astype(F32)
    centred = rows - jnp.mean(rows, axis=-1, keepdims=True)
    var = jnp.mean(centred * centred, axis=-1, keepdims=True)
    normed = (centred * lax.rsqrt(var + EPS) * gain[...]).astype(BF16)
    weights_in[1].wait()
    half = 0.5 * jnp.dot(normed, weight[1], preferred_element_type=F32)
    query = (silu_of_half(half) * HALF_SCALE).astype(BF16)
    for j in range(heads):
        queries[j][...] = query[:, j * DH : (j + 1) * DH]
    weights_in[0].wait()
    half = 0.5 * jnp.dot(normed, weight[0], preferred_element_type=F32)
    gate_ref[...] = silu_of_half(half).astype(BF16)


def project(candidates, input_gain, proj_weight, slot_user, slot_block, history_len, block_len):
    rows, cols = candidates.shape[1], proj_weight.shape[2]
    slots = slot_user.shape[0]
    heads = cols // DH
    width = -(-(slots + UNIT) // 128) * 128
    outs = pl.pallas_call(
        functools.partial(project_kernel, block_len),
        out_shape=[jax.ShapeDtypeStruct((rows, DH), BF16)] * heads
        + [jax.ShapeDtypeStruct((rows, cols), BF16), jax.ShapeDtypeStruct((4, width), jnp.int32)],
        in_specs=[HB] * 6,
        out_specs=[VM] * (heads + 1) + [SM],
        scratch_shapes=[
            pltpu.VMEM(candidates.shape, BF16),
            pltpu.VMEM((1, D), F32),
            pltpu.VMEM(proj_weight.shape, BF16),
            pltpu.SMEM(slot_user.shape, jnp.int32),
            pltpu.SMEM(slot_block.shape, jnp.int32),
            pltpu.SMEM(history_len.shape, jnp.int32),
            pltpu.SemaphoreType.DMA((5,)),
            pltpu.SemaphoreType.DMA((2,)),
        ],
        compiler_params=params(),
        cost_estimate=pl.CostEstimate(
            flops=4 * rows * cols * D, bytes_accessed=6 * cols * D, transcendentals=2 * rows * cols
        ),
        name="project",
    )(candidates, input_gain, proj_weight, slot_user, slot_block, history_len)
    return outs[:heads], outs[heads], outs[heads + 1]


def attend_kernel(head, which, users, afters, plan, *refs):
    queries, cache, outs = refs[:users], refs[users], refs[users + afters + 1 : -5]
    held, total, kv, wts, sems = refs[-5:]
    block_len = cache.shape[2]
    half = block_len // 2
    start = plan[COUNT, 0] if which == "even" else 0
    stop = plan[COUNT, 0] if which == "odd" else plan[COUNT, 1]
    steps = (stop - start + UNIT - 1) // UNIT

    def fetch(u, g):
        buf = lax.rem(u, BUFS)
        slot = plan[SLOT, start + u * UNIT + g]
        return pltpu.make_async_copy(cache.at[slot, head], kv.at[buf, g], sems.at[buf, g])

    def place(u, g):
        off = plan[OFFSET, start + u * UNIT + g]
        return off if which == "all" else off // 2

    for u in range(BUFS):

        @pl.when(u < steps)
        def _():
            for g in range(UNIT):
                fetch(jnp.int32(u), g).start()

    for d in range(users):
        held[d] = queries[d][...]
    total[...] = jnp.zeros_like(total)

    def arrive(u):
        buf = lax.rem(u, BUFS)
        for g in range(UNIT):
            fetch(u, g).wait()
            at = start + u * UNIT + g
            live = jnp.where(at < stop, plan[LIVE, at], 0)

            @pl.when(live < block_len)
            def _():
                event = lax.broadcasted_iota(jnp.int32, (block_len, DH), 0)
                vals = kv[buf, g, :, DH:]
                kv[buf, g, :, DH:] = jnp.where(event < live, vals, jnp.zeros_like(vals))

    def weigh(u, g, e):
        buf = lax.rem(u, BUFS)
        scores = lax.dot_general(
            held[place(u, g)],
            kv[buf, g, e * half : (e + 1) * half, :DH],
            (((1,), (1,)), ((), ())),
            preferred_element_type=F32,
        )
        wts[g, e] = silu_of_half(scores).astype(BF16)

    def value(u, g, e):
        buf = lax.rem(u, BUFS)
        return jnp.dot(
            wts[g, e], kv[buf, g, e * half : (e + 1) * half, DH:], preferred_element_type=F32
        )

    def gather(u, then):
        for g in range(UNIT):
            acc = value(u, g, 0)
            then(g, 0)
            acc = acc + value(u, g, 1)
            then(g, 1)
            total[place(u, g)] += acc

    @pl.when(steps > 0)
    def _():
        arrive(jnp.int32(0))
        for g in range(UNIT):
            for e in range(2):
                weigh(jnp.int32(0), g, e)

        def step(u, carry):
            arrive(u)
            gather(u - 1, lambda g, e: weigh(u, g, e))

            @pl.when(u - 1 + BUFS < steps)
            def _():
                for g in range(UNIT):
                    fetch(u - 1 + BUFS, g).start()

            return carry

        lax.fori_loop(1, steps, step, 0)
        gather(steps - 1, lambda g, e: None)

    if which == "all":
        near, far = outs
        for d in range(users):
            if d % 2 == 0:
                near[d // 2] = total[d]
            else:
                far[d // 2] = total[d].astype(BF16)
    else:
        outs[0][...] = total[...].astype(outs[0].dtype)


def attend(queries, history_cache, plan, head, which, after):
    users = len(queries)
    rows = queries[0].shape[0]
    slots, _, block_len, width = history_cache.shape
    near = jax.ShapeDtypeStruct((users // (2 if which == "all" else 1), rows, DH), F32)
    far = jax.ShapeDtypeStruct(near.shape, BF16)
    outs = {"all": [near, far], "even": [near], "odd": [far]}[which]
    share = 1 if which == "all" else 2
    return pl.pallas_call(
        functools.partial(attend_kernel, head, which, users, len(after)),
        out_shape=outs,
        in_specs=[SM] + [VM] * users + [HB] + [ANY] * len(after),
        out_specs=[VM] * len(outs),
        scratch_shapes=[
            pltpu.VMEM((users, rows, DH), BF16),
            pltpu.VMEM((users, rows, DH), F32),
            pltpu.VMEM((BUFS, UNIT, block_len, width), BF16),
            pltpu.VMEM((UNIT, 2, rows, block_len // 2), BF16),
            pltpu.SemaphoreType.DMA((BUFS, UNIT)),
        ],
        compiler_params=params(),
        cost_estimate=pl.CostEstimate(
            flops=2 * slots * rows * block_len * width // share,
            bytes_accessed=2 * slots * block_len * width // share,
            transcendentals=slots * rows * block_len // share,
        ),
        name=f"attend_{head}_{which}",
    )(plan, *queries, history_cache, *after)


def pair_kernel(chips, near, far, *refs):
    own, *sends = refs[-chips:]
    own[...] = near[0] + far[0].astype(F32)
    for e, send in enumerate(sends, 1):
        send[...] = (near[e] + far[e].astype(F32)).astype(BF16)


def pair_terms(near, far, after):
    chips, rows, cols = near.shape
    outs = [jax.ShapeDtypeStruct((rows, cols), F32)]
    outs += [jax.ShapeDtypeStruct((rows, cols), BF16)] * (chips - 1)
    return pl.pallas_call(
        functools.partial(pair_kernel, chips),
        out_shape=outs,
        in_specs=[VM] * 2 + [ANY] * len(after),
        out_specs=[VM] * chips,
        compiler_params=params(),
        name="pair_terms",
    )(near, far, *after)


def add_kernel(*refs):
    acc = refs[0][...]
    for ref in refs[1:-1]:
        acc = acc + ref[...].astype(F32)
    refs[-1][...] = acc.astype(BF16)


def add_terms(terms):
    return pl.pallas_call(
        add_kernel,
        out_shape=jax.ShapeDtypeStruct(terms[0].shape, BF16),
        in_specs=[VM] * len(terms),
        out_specs=VM,
        compiler_params=params(),
        name="add_terms",
    )(*terms)


def finish_kernel(shape, cand_ref, gain_ref, weight_ref, *refs):
    parts = len(shape)
    out_ref, refs = refs[-1], list(refs[:-1])
    gate = [refs.pop(0) for _ in range(parts)]
    blocks = [
        jnp.concatenate(
            [sum(refs.pop(0)[...].astype(F32) for _ in range(n)) for n in counts], axis=-1
        )
        for counts in shape
    ]
    me = lax.axis_index("hist")
    cols = out_ref.shape[2]
    mean = sum(jnp.sum(b, axis=-1, keepdims=True) for b in blocks) / D
    blocks = [b - mean for b in blocks]
    var = sum(jnp.sum(b * b, axis=-1, keepdims=True) for b in blocks) / D
    rstd = lax.rsqrt(var + EPS)
    acc = cand_ref[0, :, pl.ds(pl.multiple_of(me * cols, DH), cols)].astype(F32)
    for k in range(parts):
        at = pl.ds(pl.multiple_of((me ^ k) * cols, DH), cols)
        gained = blocks[k] * rstd * gain_ref[:, at]
        gated = (gained * gate[k][...].astype(F32)).astype(BF16)
        acc = acc + jnp.dot(gated, weight_ref[at, :], preferred_element_type=F32)
    out_ref[0] = acc.astype(BF16)


def finish(candidates, attention_gain, out_weight, gate, attn):
    rows, cols = gate[0].shape
    shape = [[len(group) for group in heads] for heads in attn]
    flat = [x for heads in attn for group in heads for x in group]
    return pl.pallas_call(
        functools.partial(finish_kernel, shape),
        out_shape=jax.ShapeDtypeStruct((1, rows, cols), BF16),
        in_specs=[VM] * (3 + len(gate) + len(flat)),
        out_specs=VM,
        compiler_params=params(),
        name="finish",
    )(candidates, attention_gain.reshape(1, D), out_weight, *gate, *flat)


def swap(x, axis, bit):
    n = lax.axis_size(axis)
    return lax.ppermute(x, axis, [(i, i ^ bit) for i in range(n)])


def exchange(x, axis):
    n = lax.axis_size(axis)
    if n != 4:
        return [[x]] + [[swap(x, axis, k)] for k in range(1, n)]
    one, two = swap(x, axis, 1), swap(x, axis, 2)
    mid = lax.ppermute(x, axis, [(1, 2), (2, 1)])
    ends = lax.ppermute(two, axis, [(2, 3), (1, 0)])
    return [[x], [one], [two], [mid, ends]]


def spread(x, users):
    near = [x] + [swap(x, "cand", d) for d in range(2, users, 2)]
    out = []
    for y in near:
        out += [y, swap(y, "cand", 1)]
    return out


def local(
    candidates,
    input_gain,
    proj_weight,
    history_cache,
    slot_user,
    slot_block,
    history_len,
    attention_gain,
    out_weight,
):
    users = lax.axis_size("cand")
    parts = lax.axis_size("hist")
    in_hbm = functools.partial(pltpu.with_memory_space_constraint, memory_space=pltpu.HBM)
    history_cache = in_hbm(history_cache)
    query_own, gate_own, plan = project(
        in_hbm(candidates),
        in_hbm(input_gain.reshape(1, D)),
        in_hbm(proj_weight),
        in_hbm(slot_user),
        in_hbm(slot_block),
        in_hbm(history_len),
        history_cache.shape[2],
    )
    heads = len(query_own)
    queries = [spread(q, users) for q in query_own]
    gate = [gate_own] + [swap(gate_own, "hist", k) for k in range(1, parts)]
    sums, after = [], []
    for j in range(heads):
        if j < heads - 1:
            near, far = attend(queries[j], history_cache, plan, j, "all", after)
        else:
            (far,) = attend(queries[j][1::2], history_cache, plan, j, "odd", after + gate[1:])
            after = [far] + [terms[0] for terms in sums[-1:]]
            (near,) = attend(queries[j][0::2], history_cache, plan, j, "even", after)
        after = [near]
        sums = [add_terms(terms) if isinstance(terms, list) else terms for terms in sums]
        terms = pair_terms(near, swap(far, "cand", 1), sums)
        sums.append([terms[0]] + [swap(t, "cand", 2 * e) for e, t in enumerate(terms[1:], 1)])
    sums[-1] = add_terms(sums[-1])
    attn = [exchange(x, "hist") for x in sums]
    attn = [[attn[j][k] for j in range(heads)] for k in range(parts)]
    return finish(candidates, attention_gain, out_weight, gate, attn)


def solution(mesh):
    return jax.shard_map(
        local,
        mesh=mesh,
        in_specs=(
            P("cand", None, None),
            P(),
            P(None, None, "hist"),
            P("cand", "hist", None, None),
            P("cand"),
            P("cand"),
            P(),
            P(),
            P(None, "hist"),
        ),
        out_specs=P("cand", None, "hist"),
        check_vma=False,
    )
```

time: 217 us -> 67.2 us (0.31)
  waiting for transfers between devices: 125 us -> 11.3 us
  matrix products: 39.4 us -> 0 us
  starting transfers between devices: 0.13 us -> 34 us
  local copies, waits for them, and re-layouts: 25.3 us -> 0.02 us
  Pallas kernels: 0 us -> 21.2 us
  between operations: 13.2 us -> 0.23 us
  other arithmetic: 12.8 us -> 0 us
    all_gather x3 -> x0, waiting for transfers between devices: 88.9 us -> none  [the longest x1 36.1 us: local(): features = lax.all_gather(normed_input, 'cand', axis=0, tiled=True)]
    dot_general x5 -> x0, matrix products: 39.4 us -> none  [the longest x1 24.6 us: local(): jnp.einsum('shct,shtd->schd', weights, cache_values, preferred_element_ty...]
    reduce_scatter x1 -> x0, waiting for transfers between devices: 36.1 us -> none  [local(): lax.psum_scatter(buffer.astype(jnp.bfloat16), 'cand', scatter_dimension=0...]
    ppermute x0 -> x33, starting transfers between devices: none -> 34 us  [the longest x29 30.1 us: swap(): return lax.ppermute(x, axis, [(i, i ^ bit) for i in range(n)])]
    pallas_call x0 -> x9, Pallas kernels: none -> 21.2 us  [the longest x3 16.6 us: attend(): pl.pallas_call(functools.partial(attend_kernel, head, which, users, len(a...]
    gather x2 -> x0, local copies, waits for them, and re-layouts: 12.5 us -> none  [local(): jnp.take(query_all, slot_user, axis=0)]
    reshape x1 -> x0, local copies, waits for them, and re-layouts: 11.6 us -> none  [local(): partial_value = partial_value.reshape(slot_count, cand_count, head_cols)]
    ppermute x0 -> x33, waiting for transfers between devices: none -> 11.3 us  [the longest x29 6.5 us: swap(): return lax.ppermute(x, axis, [(i, i ^ bit) for i in range(n)])]
  transfers between devices with their start and end apart: 4 -> 33, of which waited for: 4 -> 6; matrix products, arithmetic and copies ran while one was open for 3% -> 0% of each run, Pallas kernels for 0% -> 25%
where the time goes in v1:
time: 67.2 us; the launch traced here: 66.8 us
  starting transfers between devices  34 us (51%)
  Pallas kernels  21.2 us (32%)
  waiting for transfers between devices  11.3 us (17%)
    ppermute x29, starting transfers between devices, swap(): return lax.ppermute(x, axis, [(i, i ^ bit) for i in range(n)])  30.1 us
    pallas_call x3, Pallas kernels, attend(): pl.pallas_call(functools.partial(attend_kernel, head, which, users, len(a...  16.6 us
    ppermute x29, waiting for transfers between devices, swap(): return lax.ppermute(x, axis, [(i, i ^ bit) for i in range(n)])  6.5 us
    ppermute x2, waiting for transfers between devices, exchange(): ends = lax.ppermute(two, axis, [(2, 3), (1, 0)])  4.84 us
    pallas_call x1, Pallas kernels, project(): pl.pallas_call(functools.partial(project_kernel, block_len), out_shape=[j...  3.11 us
    ppermute x2, starting transfers between devices, exchange(): ends = lax.ppermute(two, axis, [(2, 3), (1, 0)])  2.58 us
  transfers between devices with their start and end apart: 33, of which 6 were waited for; matrix products, arithmetic and copies ran while one was open for 0% of the time, Pallas kernels for 25%

profile of v1, /device:TPU:0, one launch (start us, length us, event | category | flops | bytes accessed | tf_op | source)
XLA Modules:
  0.0 66.8 jit_solution(10980938448573378317)
XLA Ops:
  0.0 3.1 %project.1 = (bf16[256,128]{1,0:T(8,128)(2,1)S(1)}, bf16[256,128]{1,0:T(8,128)(2,1)S(1)}, bf16[256,256]{1,0:T(8,128)(2,1)S(1)}, s32[4,128]{1,0:T(4,128)S(1)}) custom-call(bf16[1,256,1024]{2,1,0:T(8,128)(2,1)} %cand_ref.1, f32[1,1024]{1,0:T(1,128)} %bitcast.3, bf16[2,1024,256]{2,1,0:T(8,128)(2,1)} %weight_hbm.1, s32[40]{0:T(128)} %user_hbm.1, s32[40]{0:T(128)} %block_hbm.1, ...), custom_call_target="tpu_custom_call" | custom-call | flops 268435456 | bytes 1572864 | tf_op jit(solution)/shard_map/project/pallas_call | solution.py:101
  3.1 0.5 collective-permute-start.3
  3.6 2.6 %collective-permute-start.4 = (bf16[256,128]{1,0:T(8,128)(2,1)S(1)}, bf16[256,128]{1,0:T(8,128)(2,1)S(1)}, u32[]{:S(2)}, u32[]{:S(2)}) collective-permute-start(bf16[256,128]{1,0:T(8,128)(2,1)S(1)} %get-tuple-element.21.refs_0_), channel_id=1, source_target_pairs={{0,2},{1,3},{2,0},{3,1},{4,6},{5,7},{6,4},{7,5},{8,10},{9,11},{10,... | collective-permute-start | bytes 196616 | tf_op jit(solution)/shard_map/ppermute | solution.py:334
  6.2 1.5 %collective-permute-start.6 = (bf16[256,128]{1,0:T(8,128)(2,1)S(1)}, bf16[256,128]{1,0:T(8,128)(2,1)S(1)}, u32[]{:S(2)}, u32[]{:S(2)}) collective-permute-start(bf16[256,128]{1,0:T(8,128)(2,1)S(1)} %get-tuple-element.21.refs_0_), channel_id=1, source_target_pairs={{0,4},{1,5},{2,6},{3,7},{4,0},{5,1},{6,2},{7,3},{8,12},{9,13},{10,... | collective-permute-start | bytes 196616 | tf_op jit(solution)/shard_map/ppermute | solution.py:334
  7.7 0.0 collective-permute-start.8
  7.7 2.0 %collective-permute-start = (bf16[256,256]{1,0:T(8,128)(2,1)S(1)}, bf16[256,256]{1,0:T(8,128)(2,1)S(1)}, u32[]{:S(2)}, u32[]{:S(2)}) collective-permute-start(bf16[256,256]{1,0:T(8,128)(2,1)S(1)} %get-tuple-element.19.refs_0_), channel_id=1, source_target_pairs={{0,8},{8,0},{16,24},{24,16},{1,9},{9,1},{17,25},{25,17},{2,10},{10... | collective-permute-start | bytes 393224 | tf_op jit(solution)/shard_map/ppermute | solution.py:334
  9.8 0.0 collective-permute-done.3.refs_1_
  9.8 1.5 %collective-permute-start.14 = (bf16[256,128]{1,0:T(8,128)(2,1)S(1)}, bf16[256,128]{1,0:T(8,128)(2,1)S(1)}, u32[]{:S(2)}, u32[]{:S(2)}) collective-permute-start(bf16[256,128]{1,0:T(8,128)(2,1)S(1)} %get-tuple-element.28.refs_0_), channel_id=1, source_target_pairs={{0,2},{1,3},{2,0},{3,1},{4,6},{5,7},{6,4},{7,5},{8,10},{9,11},{10,... | collective-permute-start | bytes 196616 | tf_op jit(solution)/shard_map/ppermute | solution.py:334
  11.3 0.0 collective-permute-done.4.refs_2_
  11.3 1.5 %collective-permute-start.15 = (bf16[256,128]{1,0:T(8,128)(2,1)S(1)}, bf16[256,128]{1,0:T(8,128)(2,1)S(1)}, u32[]{:S(2)}, u32[]{:S(2)}) collective-permute-start(bf16[256,128]{1,0:T(8,128)(2,1)S(1)} %get-tuple-element.28.refs_0_), channel_id=1, source_target_pairs={{0,4},{1,5},{2,6},{3,7},{4,0},{5,1},{6,2},{7,3},{8,12},{9,13},{10,... | collective-permute-start | bytes 196616 | tf_op jit(solution)/shard_map/ppermute | solution.py:334
  12.8 0.0 collective-permute-done.6.refs_4_
  12.8 0.6 collective-permute-start.16
  13.4 0.0 collective-permute-start.17
  13.4 0.7 %collective-permute-done.14.refs_1_ = bf16[256,128]{1,0:T(8,128)(2,1)S(1)} collective-permute-done((bf16[256,128]{1,0:T(8,128)(2,1)S(1)}, bf16[256,128]{1,0:T(8,128)(2,1)S(1)}, u32[]{:S(2)}, u32[]{:S(2)}) %collective-permute-start.14) | collective-permute-done | bytes 65568 | tf_op jit(solution)/shard_map/ppermute | solution.py:334
  14.0 0.0 collective-permute-start.5
  14.1 2.2 %collective-permute-done.15.refs_2_ = bf16[256,128]{1,0:T(8,128)(2,1)S(1)} collective-permute-done((bf16[256,128]{1,0:T(8,128)(2,1)S(1)}, bf16[256,128]{1,0:T(8,128)(2,1)S(1)}, u32[]{:S(2)}, u32[]{:S(2)}) %collective-permute-start.15) | collective-permute-done | bytes 65568 | tf_op jit(solution)/shard_map/ppermute | solution.py:334
  16.2 0.0 collective-permute-start.7
  16.2 1.7 %collective-permute-done.16.refs_3_ = bf16[256,128]{1,0:T(8,128)(2,1)S(1)} collective-permute-done((bf16[256,128]{1,0:T(8,128)(2,1)S(1)}, bf16[256,128]{1,0:T(8,128)(2,1)S(1)}, u32[]{:S(2)}, u32[]{:S(2)}) %collective-permute-start.16) | collective-permute-done | bytes 65568 | tf_op jit(solution)/shard_map/ppermute | solution.py:334
  18.0 2.6 %collective-permute-start.1 = (bf16[256,256]{1,0:T(8,128)(2,1)S(1)}, bf16[256,256]{1,0:T(8,128)(2,1)S(1)}, u32[]{:S(2)}, u32[]{:S(2)}) collective-permute-start(bf16[256,256]{1,0:T(8,128)(2,1)S(1)} %get-tuple-element.19.refs_0_), channel_id=1, source_target_pairs={{0,16},{8,24},{16,0},{24,8},{1,17},{9,25},{17,1},{25,9},{2,18},{10... | collective-permute-start | bytes 393224 | tf_op jit(solution)/shard_map/ppermute | solution.py:334
  20.6 0.0 collective-permute-done.refs_6_.refs_1_
  20.6 0.2 collective-permute-start.2
  20.8 0.1 collective-permute-start.18
  20.9 0.0 collective-permute-done.7.refs_5_
  20.9 0.4 collective-permute-start.19
  21.3 0.1 collective-permute-start.20
  21.4 7.1 %attend_0_all.1 = (f32[4,256,128]{2,1,0:T(8,128)S(1)}, bf16[4,256,128]{2,1,0:T(8,128)(2,1)S(1)}) custom-call(s32[4,128]{1,0:T(4,128)S(1)} %get-tuple-element.20.plan, bf16[256,128]{1,0:T(8,128)(2,1)S(1)} %get-tuple-element.21.refs_0_, bf16[256,128]{1,0:T(8,128)(2,1)S(1)} %collective-permute-done.3.refs_1_, ...), custom_call_target="tpu_custom_call" | custom-call | flops 2684354560 | bytes 10485760 | tf_op jit(solution)/shard_map/attend_0_all/pallas_call | solution.py:232
  28.5 1.8 %collective-permute-done.1.refs_7_.refs_2_ = bf16[256,256]{1,0:T(8,128)(2,1)S(1)} collective-permute-done((bf16[256,256]{1,0:T(8,128)(2,1)S(1)}, bf16[256,256]{1,0:T(8,128)(2,1)S(1)}, u32[]{:S(2)}, u32[]{:S(2)}) %collective-permute-start.1) | collective-permute-done | bytes 131104 | tf_op jit(solution)/shard_map/ppermute | solution.py:334
  30.3 0.0 collective-permute-start.10
  30.4 0.0 collective-permute-done.20.refs_3_
  30.4 0.0 copy-start
  30.4 0.0 copy-start.1
  30.4 0.0 copy-start.2
  30.4 4.3 %attend_1_odd.1.refs_5_ = bf16[4,256,128]{2,1,0:T(8,128)(2,1)S(1)} custom-call(s32[4,128]{1,0:T(4,128)S(1)} %get-tuple-element.20.plan, bf16[256,128]{1,0:T(8,128)(2,1)S(1)} %collective-permute-done.17.refs_0_, bf16[256,128]{1,0:T(8,128)(2,1)S(1)} %collective-permute-done.18.refs_1_, bf16[256,128]{1,0:T(8,128)(2,1)S(1)} %collective-permute-done.19.refs_2_, ...), custom_call_target="tpu_custom_call" | custom-call | flops 1342177280 | bytes 5242880 | tf_op jit(solution)/shard_map/attend_1_odd/pallas_call | solution.py:232
  34.7 0.1 collective-permute-start.21
  34.8 0.0 collective-permute-done.10.far
  34.8 0.1 pair_terms.2
  34.8 1.0 %collective-permute-start.11 = (bf16[256,128]{1,0:T(8,128)(2,1)S(1)}, bf16[256,128]{1,0:T(8,128)(2,1)S(1)}, u32[]{:S(2)}, u32[]{:S(2)}) collective-permute-start(bf16[256,128]{1,0:T(8,128)(2,1)S(1)} %get-tuple-element.25), channel_id=1, source_target_pairs={{0,2},{1,3},{2,0},{3,1},{4,6},{5,7},{6,4},{7,5},{8,10},{9,11},{10,... | collective-permute-start | bytes 196616 | tf_op jit(solution)/shard_map/ppermute | solution.py:334
  35.9 1.0 %collective-permute-start.12 = (bf16[256,128]{1,0:T(8,128)(2,1)S(1)}, bf16[256,128]{1,0:T(8,128)(2,1)S(1)}, u32[]{:S(2)}, u32[]{:S(2)}) collective-permute-start(bf16[256,128]{1,0:T(8,128)(2,1)S(1)} %get-tuple-element.26), channel_id=1, source_target_pairs={{0,4},{1,5},{2,6},{3,7},{4,0},{5,1},{6,2},{7,3},{8,12},{9,13},{10,... | collective-permute-start | bytes 196616 | tf_op jit(solution)/shard_map/ppermute | solution.py:334
  36.9 1.5 %collective-permute-start.13 = (bf16[256,128]{1,0:T(8,128)(2,1)S(1)}, bf16[256,128]{1,0:T(8,128)(2,1)S(1)}, u32[]{:S(2)}, u32[]{:S(2)}) collective-permute-start(bf16[256,128]{1,0:T(8,128)(2,1)S(1)} %get-tuple-element.27), channel_id=1, source_target_pairs={{0,6},{1,7},{2,4},{3,5},{4,2},{5,3},{6,0},{7,1},{8,14},{9,15},{10,... | collective-permute-start | bytes 196616 | tf_op jit(solution)/shard_map/ppermute | solution.py:334
  38.4 5.2 %attend_1_even.1.near = f32[4,256,128]{2,1,0:T(8,128)S(1)} custom-call(s32[4,128]{1,0:T(4,128)S(1)} %get-tuple-element.20.plan, bf16[256,128]{1,0:T(8,128)(2,1)S(1)} %get-tuple-element.28.refs_0_, bf16[256,128]{1,0:T(8,128)(2,1)S(1)} %collective-permute-done.14.refs_1_, bf16[256,128]{1,0:T(8,128)(2,1)S(1)} %collective-permute-done.15.refs_2_, ...), custom_call_target="tpu_custom_call" | custom-call | flops 1342177280 | bytes 5242880 | tf_op jit(solution)/shard_map/attend_1_even/pallas_call | solution.py:232
  43.6 0.0 collective-permute-done.11.refs_1_
  43.6 0.0 collective-permute-done.12.refs_2_
  43.7 0.0 collective-permute-done.21.far
  43.7 0.1 pair_terms.3
  43.8 0.1 collective-permute-start.22
  43.9 1.0 %collective-permute-start.23 = (bf16[256,128]{1,0:T(8,128)(2,1)S(1)}, bf16[256,128]{1,0:T(8,128)(2,1)S(1)}, u32[]{:S(2)}, u32[]{:S(2)}) collective-permute-start(bf16[256,128]{1,0:T(8,128)(2,1)S(1)} %get-tuple-element.31), channel_id=1, source_target_pairs={{0,4},{1,5},{2,6},{3,7},{4,0},{5,1},{6,2},{7,3},{8,12},{9,13},{10,... | collective-permute-start | bytes 196616 | tf_op jit(solution)/shard_map/ppermute | solution.py:334
  44.8 2.5 %collective-permute-start.24 = (bf16[256,128]{1,0:T(8,128)(2,1)S(1)}, bf16[256,128]{1,0:T(8,128)(2,1)S(1)}, u32[]{:S(2)}, u32[]{:S(2)}) collective-permute-start(bf16[256,128]{1,0:T(8,128)(2,1)S(1)} %get-tuple-element.32), channel_id=1, source_target_pairs={{0,6},{1,7},{2,4},{3,5},{4,2},{5,3},{6,0},{7,1},{8,14},{9,15},{10,... | collective-permute-start | bytes 196616 | tf_op jit(solution)/shard_map/ppermute | solution.py:334
  47.3 3.3 %collective-permute-start.25 = (bf16[256,128]{1,0:T(8,128)(2,1)S(1)}, bf16[256,128]{1,0:T(8,128)(2,1)S(1)}, u32[]{:S(2)}, u32[]{:S(2)}) collective-permute-start(bf16[256,128]{1,0:T(8,128)(2,1)S(1)} %add_terms.2.refs_0_.refs_4_), channel_id=1, source_target_pairs={{0,8},{8,0},{16,24},{24,16},{1,9},{9,1},{17,25},{25,17},{2,10},{10... | collective-permute-start | bytes 196616 | tf_op jit(solution)/shard_map/ppermute | solution.py:334
  50.6 1.1 %collective-permute-start.27 = (bf16[256,128]{1,0:T(8,128)(2,1)S(1)}, bf16[256,128]{1,0:T(8,128)(2,1)S(1)}, u32[]{:S(2)}, u32[]{:S(2)}) collective-permute-start(bf16[256,128]{1,0:T(8,128)(2,1)S(1)} %add_terms.2.refs_0_.refs_4_), channel_id=1, source_target_pairs={{0,16},{8,24},{16,0},{24,8},{1,17},{9,25},{17,1},{25,9},{2,18},{10... | collective-permute-start | bytes 196616 | tf_op jit(solution)/shard_map/ppermute | solution.py:334
  51.7 0.0 collective-permute-done.22.refs_1_
  51.7 0.0 collective-permute-done.23.refs_2_
  51.8 2.7 %collective-permute-start.28 = (bf16[256,128]{1,0:T(8,128)(2,1)S(1)}, bf16[256,128]{1,0:T(8,128)(2,1)S(1)}, u32[]{:S(2)}, u32[]{:S(2)}) collective-permute-start(bf16[256,128]{1,0:T(8,128)(2,1)S(1)} %add_terms.3.refs_5_), channel_id=1, source_target_pairs={{0,16},{8,24},{16,0},{24,8},{1,17},{9,25},{17,1},{25,9},{2,18},{10... | collective-permute-start | bytes 196616 | tf_op jit(solution)/shard_map/ppermute | solution.py:334
  54.5 0.7 collective-permute-start.29
  55.2 2.1 %collective-permute-start.26 = (bf16[256,128]{1,0:T(8,128)(2,1)S(1)}, bf16[256,128]{1,0:T(8,128)(2,1)S(1)}, u32[]{:S(2)}, u32[]{:S(2)}) collective-permute-start(bf16[256,128]{1,0:T(8,128)(2,1)S(1)} %add_terms.3.refs_5_), channel_id=1, source_target_pairs={{0,8},{8,0},{16,24},{24,16},{1,9},{9,1},{17,25},{25,17},{2,10},{10... | collective-permute-start | bytes 196616 | tf_op jit(solution)/shard_map/ppermute | solution.py:334
  57.3 0.0 collective-permute-done.25.refs_6_
  57.3 0.7 collective-permute-start.31
  58.0 0.0 collective-permute-done.27.refs_8_
  58.0 1.3 %collective-permute-start.30 = (bf16[256,128]{1,0:T(8,128)(2,1)S(1)}, bf16[256,128]{1,0:T(8,128)(2,1)S(1)}, u32[]{:S(2)}, u32[]{:S(2)}) collective-permute-start(bf16[256,128]{1,0:T(8,128)(2,1)S(1)} %collective-permute-done.27.refs_8_), channel_id=1, source_target_pairs={{16,24},{8,0},{17,25},{9,1},{18,26},{10,2},{19,27},{11,3},{20,28},... | collective-permute-start | bytes 196616 | tf_op jit(solution)/shard_map/ppermute | solution.py:343
  59.3 0.0 collective-permute-done.28.refs_9_
  59.3 1.3 %collective-permute-start.32 = (bf16[256,128]{1,0:T(8,128)(2,1)S(1)}, bf16[256,128]{1,0:T(8,128)(2,1)S(1)}, u32[]{:S(2)}, u32[]{:S(2)}) collective-permute-start(bf16[256,128]{1,0:T(8,128)(2,1)S(1)} %collective-permute-done.28.refs_9_), channel_id=1, source_target_pairs={{16,24},{8,0},{17,25},{9,1},{18,26},{10,2},{19,27},{11,3},{20,28},... | collective-permute-start | bytes 196616 | tf_op jit(solution)/shard_map/ppermute | solution.py:343
  60.6 0.0 collective-permute-done.26.refs_7_
  60.6 3.5 %collective-permute-done.30.refs_11_ = bf16[256,128]{1,0:T(8,128)(2,1)S(1)} collective-permute-done((bf16[256,128]{1,0:T(8,128)(2,1)S(1)}, bf16[256,128]{1,0:T(8,128)(2,1)S(1)}, u32[]{:S(2)}, u32[]{:S(2)}) %collective-permute-start.30) | collective-permute-done | bytes 65568 | tf_op jit(solution)/shard_map/ppermute | solution.py:343
  64.2 1.3 %collective-permute-done.32.refs_13_ = bf16[256,128]{1,0:T(8,128)(2,1)S(1)} collective-permute-done((bf16[256,128]{1,0:T(8,128)(2,1)S(1)}, bf16[256,128]{1,0:T(8,128)(2,1)S(1)}, u32[]{:S(2)}, u32[]{:S(2)}) %collective-permute-start.32) | collective-permute-done | bytes 65568 | tf_op jit(solution)/shard_map/ppermute | solution.py:343
  65.5 1.3 %finish.1 = bf16[1,256,256]{2,1,0:T(8,128)(2,1)} custom-call(bf16[1,256,1024]{2,1,0:T(8,128)(2,1)S(1)} %copy-done, f32[1,1024]{1,0:T(1,128)S(1)} %bitcast.2, bf16[1024,256]{1,0:T(8,128)(2,1)S(1)} %copy-done.1, bf16[256,256]{1,0:T(8,128)(2,1)S(1)} %get-tuple-element.19.refs_0_, bf16[256,256]{1,0:T(8,128)(2,1)S(1)} %collective-permute-done.refs_6_.refs_1_, ...), custom_call_target="tpu_custom_call" | custom-call | tf_op jit(solution)/shard_map/finish/pallas_call | solution.py:322
  (17 shorter events, 0.1 us)
Async XLA Ops:
  3.1 6.7 %collective-permute-start.3 = (bf16[256,128]{1,0:T(8,128)(2,1)S(1)}, bf16[256,128]{1,0:T(8,128)(2,1)S(1)}, u32[]{:S(2)}, u32[]{:S(2)}) collective-permute-start(bf16[256,128]{1,0:T(8,128)(2,1)S(1)} %get-tuple-element.21.refs_0_), channel_id=1, source_target_pairs={{0,1},{1,0},{2,3},{3,2},{4,5},{5,4},{6,7},{7,6},{8,9},{9,8},{10,11... | collective-permute-start | bytes 196616 | tf_op jit(solution)/shard_map/ppermute | solution.py:334
  3.6 7.6 %collective-permute-start.4 = (bf16[256,128]{1,0:T(8,128)(2,1)S(1)}, bf16[256,128]{1,0:T(8,128)(2,1)S(1)}, u32[]{:S(2)}, u32[]{:S(2)}) collective-permute-start(bf16[256,128]{1,0:T(8,128)(2,1)S(1)} %get-tuple-element.21.refs_0_), channel_id=1, source_target_pairs={{0,2},{1,3},{2,0},{3,1},{4,6},{5,7},{6,4},{7,5},{8,10},{9,11},{10,... | collective-permute-start | bytes 196616 | tf_op jit(solution)/shard_map/ppermute | solution.py:334
  6.2 6.6 %collective-permute-start.6 = (bf16[256,128]{1,0:T(8,128)(2,1)S(1)}, bf16[256,128]{1,0:T(8,128)(2,1)S(1)}, u32[]{:S(2)}, u32[]{:S(2)}) collective-permute-start(bf16[256,128]{1,0:T(8,128)(2,1)S(1)} %get-tuple-element.21.refs_0_), channel_id=1, source_target_pairs={{0,4},{1,5},{2,6},{3,7},{4,0},{5,1},{6,2},{7,3},{8,12},{9,13},{10,... | collective-permute-start | bytes 196616 | tf_op jit(solution)/shard_map/ppermute | solution.py:334
  7.7 5.6 %collective-permute-start.8 = (bf16[256,128]{1,0:T(8,128)(2,1)S(1)}, bf16[256,128]{1,0:T(8,128)(2,1)S(1)}, u32[]{:S(2)}, u32[]{:S(2)}) collective-permute-start(bf16[256,128]{1,0:T(8,128)(2,1)S(1)} %get-tuple-element.21.refs_0_), channel_id=1, source_target_pairs={{0,6},{1,7},{2,4},{3,5},{4,2},{5,3},{6,0},{7,1},{8,14},{9,15},{10,... | collective-permute-start | bytes 196616 | tf_op jit(solution)/shard_map/ppermute | solution.py:334
  7.7 12.8 %collective-permute-start = (bf16[256,256]{1,0:T(8,128)(2,1)S(1)}, bf16[256,256]{1,0:T(8,128)(2,1)S(1)}, u32[]{:S(2)}, u32[]{:S(2)}) collective-permute-start(bf16[256,256]{1,0:T(8,128)(2,1)S(1)} %get-tuple-element.19.refs_0_), channel_id=1, source_target_pairs={{0,8},{8,0},{16,24},{24,16},{1,9},{9,1},{17,25},{25,17},{2,10},{10... | collective-permute-start | bytes 393224 | tf_op jit(solution)/shard_map/ppermute | solution.py:334
  9.8 4.3 %collective-permute-start.14 = (bf16[256,128]{1,0:T(8,128)(2,1)S(1)}, bf16[256,128]{1,0:T(8,128)(2,1)S(1)}, u32[]{:S(2)}, u32[]{:S(2)}) collective-permute-start(bf16[256,128]{1,0:T(8,128)(2,1)S(1)} %get-tuple-element.28.refs_0_), channel_id=1, source_target_pairs={{0,2},{1,3},{2,0},{3,1},{4,6},{5,7},{6,4},{7,5},{8,10},{9,11},{10,... | collective-permute-start | bytes 196616 | tf_op jit(solution)/shard_map/ppermute | solution.py:334
  11.3 5.0 %collective-permute-start.15 = (bf16[256,128]{1,0:T(8,128)(2,1)S(1)}, bf16[256,128]{1,0:T(8,128)(2,1)S(1)}, u32[]{:S(2)}, u32[]{:S(2)}) collective-permute-start(bf16[256,128]{1,0:T(8,128)(2,1)S(1)} %get-tuple-element.28.refs_0_), channel_id=1, source_target_pairs={{0,4},{1,5},{2,6},{3,7},{4,0},{5,1},{6,2},{7,3},{8,12},{9,13},{10,... | collective-permute-start | bytes 196616 | tf_op jit(solution)/shard_map/ppermute | solution.py:334
  12.8 5.2 %collective-permute-start.16 = (bf16[256,128]{1,0:T(8,128)(2,1)S(1)}, bf16[256,128]{1,0:T(8,128)(2,1)S(1)}, u32[]{:S(2)}, u32[]{:S(2)}) collective-permute-start(bf16[256,128]{1,0:T(8,128)(2,1)S(1)} %get-tuple-element.28.refs_0_), channel_id=1, source_target_pairs={{0,6},{1,7},{2,4},{3,5},{4,2},{5,3},{6,0},{7,1},{8,14},{9,15},{10,... | collective-permute-start | bytes 196616 | tf_op jit(solution)/shard_map/ppermute | solution.py:334
  13.4 4.6 %collective-permute-start.17 = (bf16[256,128]{1,0:T(8,128)(2,1)S(1)}, bf16[256,128]{1,0:T(8,128)(2,1)S(1)}, u32[]{:S(2)}, u32[]{:S(2)}) collective-permute-start(bf16[256,128]{1,0:T(8,128)(2,1)S(1)} %get-tuple-element.28.refs_0_), channel_id=1, source_target_pairs={{0,1},{1,0},{2,3},{3,2},{4,5},{5,4},{6,7},{7,6},{8,9},{9,8},{10,11... | collective-permute-start | bytes 196616 | tf_op jit(solution)/shard_map/ppermute | solution.py:334
  14.0 6.7 %collective-permute-start.5 = (bf16[256,128]{1,0:T(8,128)(2,1)S(1)}, bf16[256,128]{1,0:T(8,128)(2,1)S(1)}, u32[]{:S(2)}, u32[]{:S(2)}) collective-permute-start(bf16[256,128]{1,0:T(8,128)(2,1)S(1)} %collective-permute-done.4.refs_2_), channel_id=1, source_target_pairs={{0,1},{1,0},{2,3},{3,2},{4,5},{5,4},{6,7},{7,6},{8,9},{9,8},{10,11... | collective-permute-start | bytes 196616 | tf_op jit(solution)/shard_map/ppermute | solution.py:334
  16.2 4.6 %collective-permute-start.7 = (bf16[256,128]{1,0:T(8,128)(2,1)S(1)}, bf16[256,128]{1,0:T(8,128)(2,1)S(1)}, u32[]{:S(2)}, u32[]{:S(2)}) collective-permute-start(bf16[256,128]{1,0:T(8,128)(2,1)S(1)} %collective-permute-done.6.refs_4_), channel_id=1, source_target_pairs={{0,1},{1,0},{2,3},{3,2},{4,5},{5,4},{6,7},{7,6},{8,9},{9,8},{10,11... | collective-permute-start | bytes 196616 | tf_op jit(solution)/shard_map/ppermute | solution.py:334
  18.0 3.3 %collective-permute-start.9 = (bf16[256,128]{1,0:T(8,128)(2,1)S(1)}, bf16[256,128]{1,0:T(8,128)(2,1)S(1)}, u32[]{:S(2)}, u32[]{:S(2)}) collective-permute-start(bf16[256,128]{1,0:T(8,128)(2,1)S(1)} %collective-permute-done.8.refs_6_), channel_id=1, source_target_pairs={{0,1},{1,0},{2,3},{3,2},{4,5},{5,4},{6,7},{7,6},{8,9},{9,8},{10,11... | collective-permute-start | bytes 196616 | tf_op jit(solution)/shard_map/ppermute | solution.py:334
  18.0 12.4 %collective-permute-start.1 = (bf16[256,256]{1,0:T(8,128)(2,1)S(1)}, bf16[256,256]{1,0:T(8,128)(2,1)S(1)}, u32[]{:S(2)}, u32[]{:S(2)}) collective-permute-start(bf16[256,256]{1,0:T(8,128)(2,1)S(1)} %get-tuple-element.19.refs_0_), channel_id=1, source_target_pairs={{0,16},{8,24},{16,0},{24,8},{1,17},{9,25},{17,1},{25,9},{2,18},{10... | collective-permute-start | bytes 393224 | tf_op jit(solution)/shard_map/ppermute | solution.py:334
  20.6 9.8 %collective-permute-start.2 = (bf16[256,256]{1,0:T(8,128)(2,1)S(1)}, bf16[256,256]{1,0:T(8,128)(2,1)S(1)}, u32[]{:S(2)}, u32[]{:S(2)}) collective-permute-start(bf16[256,256]{1,0:T(8,128)(2,1)S(1)} %get-tuple-element.19.refs_0_), channel_id=1, source_target_pairs={{0,24},{8,16},{16,8},{24,0},{1,25},{9,17},{17,9},{25,1},{2,26},{10... | collective-permute-start | bytes 393224 | tf_op jit(solution)/shard_map/ppermute | solution.py:334
  20.8 9.6 %collective-permute-start.18 = (bf16[256,128]{1,0:T(8,128)(2,1)S(1)}, bf16[256,128]{1,0:T(8,128)(2,1)S(1)}, u32[]{:S(2)}, u32[]{:S(2)}) collective-permute-start(bf16[256,128]{1,0:T(8,128)(2,1)S(1)} %collective-permute-done.14.refs_1_), channel_id=1, source_target_pairs={{0,1},{1,0},{2,3},{3,2},{4,5},{5,4},{6,7},{7,6},{8,9},{9,8},{10,11... | collective-permute-start | bytes 196616 | tf_op jit(solution)/shard_map/ppermute | solution.py:334
  20.9 9.5 %collective-permute-start.19 = (bf16[256,128]{1,0:T(8,128)(2,1)S(1)}, bf16[256,128]{1,0:T(8,128)(2,1)S(1)}, u32[]{:S(2)}, u32[]{:S(2)}) collective-permute-start(bf16[256,128]{1,0:T(8,128)(2,1)S(1)} %collective-permute-done.15.refs_2_), channel_id=1, source_target_pairs={{0,1},{1,0},{2,3},{3,2},{4,5},{5,4},{6,7},{7,6},{8,9},{9,8},{10,11... | collective-permute-start | bytes 196616 | tf_op jit(solution)/shard_map/ppermute | solution.py:334
  21.3 9.1 %collective-permute-start.20 = (bf16[256,128]{1,0:T(8,128)(2,1)S(1)}, bf16[256,128]{1,0:T(8,128)(2,1)S(1)}, u32[]{:S(2)}, u32[]{:S(2)}) collective-permute-start(bf16[256,128]{1,0:T(8,128)(2,1)S(1)} %collective-permute-done.16.refs_3_), channel_id=1, source_target_pairs={{0,1},{1,0},{2,3},{3,2},{4,5},{5,4},{6,7},{7,6},{8,9},{9,8},{10,11... | collective-permute-start | bytes 196616 | tf_op jit(solution)/shard_map/ppermute | solution.py:334
  30.3 4.4 %collective-permute-start.10 = (bf16[4,256,128]{2,1,0:T(8,128)(2,1)S(1)}, bf16[4,256,128]{2,1,0:T(8,128)(2,1)S(1)}, u32[]{:S(2)}, u32[]{:S(2)}) collective-permute-start(bf16[4,256,128]{2,1,0:T(8,128)(2,1)S(1)} %get-tuple-element.23), channel_id=1, source_target_pairs={{0,1},{1,0},{2,3},{3,2},{4,5},{5,4},{6,7},{7,6},{8,9},{9,8},{10,11... | collective-permute-start | bytes 786440 | tf_op jit(solution)/shard_map/ppermute | solution.py:334
  30.4 35.1 %copy-start = (bf16[1,256,1024]{2,1,0:T(8,128)(2,1)S(1)}, bf16[1,256,1024]{2,1,0:T(8,128)(2,1)}, u32[]{:S(2)}) copy-start(bf16[1,256,1024]{2,1,0:T(8,128)(2,1)} %cand_ref.1) | copy-start | bytes 1572868
  30.4 35.1 %copy-start.1 = (bf16[1024,256]{1,0:T(8,128)(2,1)S(1)}, bf16[1024,256]{1,0:T(8,128)(2,1)}, u32[]{:S(2)}) copy-start(bf16[1024,256]{1,0:T(8,128)(2,1)} %weight_ref.1) | copy-start | bytes 1572868
  30.4 35.1 %copy-start.2 = (f32[1024]{0:T(1024)S(1)}, f32[1024]{0:T(1024)}, u32[]{:S(2)}) copy-start(f32[1024]{0:T(1024)} %param.16) | copy-start | bytes 12292
  34.7 9.0 %collective-permute-start.21 = (bf16[4,256,128]{2,1,0:T(8,128)(2,1)S(1)}, bf16[4,256,128]{2,1,0:T(8,128)(2,1)S(1)}, u32[]{:S(2)}, u32[]{:S(2)}) collective-permute-start(bf16[4,256,128]{2,1,0:T(8,128)(2,1)S(1)} %attend_1_odd.1.refs_5_), channel_id=1, source_target_pairs={{0,1},{1,0},{2,3},{3,2},{4,5},{5,4},{6,7},{7,6},{8,9},{9,8},{10,11... | collective-permute-start | bytes 786440 | tf_op jit(solution)/shard_map/ppermute | solution.py:334
  34.8 8.8 %collective-permute-start.11 = (bf16[256,128]{1,0:T(8,128)(2,1)S(1)}, bf16[256,128]{1,0:T(8,128)(2,1)S(1)}, u32[]{:S(2)}, u32[]{:S(2)}) collective-permute-start(bf16[256,128]{1,0:T(8,128)(2,1)S(1)} %get-tuple-element.25), channel_id=1, source_target_pairs={{0,2},{1,3},{2,0},{3,1},{4,6},{5,7},{6,4},{7,5},{8,10},{9,11},{10,... | collective-permute-start | bytes 196616 | tf_op jit(solution)/shard_map/ppermute | solution.py:334
  35.9 7.8 %collective-permute-start.12 = (bf16[256,128]{1,0:T(8,128)(2,1)S(1)}, bf16[256,128]{1,0:T(8,128)(2,1)S(1)}, u32[]{:S(2)}, u32[]{:S(2)}) collective-permute-start(bf16[256,128]{1,0:T(8,128)(2,1)S(1)} %get-tuple-element.26), channel_id=1, source_target_pairs={{0,4},{1,5},{2,6},{3,7},{4,0},{5,1},{6,2},{7,3},{8,12},{9,13},{10,... | collective-permute-start | bytes 196616 | tf_op jit(solution)/shard_map/ppermute | solution.py:334
  36.9 6.8 %collective-permute-start.13 = (bf16[256,128]{1,0:T(8,128)(2,1)S(1)}, bf16[256,128]{1,0:T(8,128)(2,1)S(1)}, u32[]{:S(2)}, u32[]{:S(2)}) collective-permute-start(bf16[256,128]{1,0:T(8,128)(2,1)S(1)} %get-tuple-element.27), channel_id=1, source_target_pairs={{0,6},{1,7},{2,4},{3,5},{4,2},{5,3},{6,0},{7,1},{8,14},{9,15},{10,... | collective-permute-start | bytes 196616 | tf_op jit(solution)/shard_map/ppermute | solution.py:334
  43.8 8.0 %collective-permute-start.22 = (bf16[256,128]{1,0:T(8,128)(2,1)S(1)}, bf16[256,128]{1,0:T(8,128)(2,1)S(1)}, u32[]{:S(2)}, u32[]{:S(2)}) collective-permute-start(bf16[256,128]{1,0:T(8,128)(2,1)S(1)} %get-tuple-element.30), channel_id=1, source_target_pairs={{0,2},{1,3},{2,0},{3,1},{4,6},{5,7},{6,4},{7,5},{8,10},{9,11},{10,... | collective-permute-start | bytes 196616 | tf_op jit(solution)/shard_map/ppermute | solution.py:334
  43.9 7.9 %collective-permute-start.23 = (bf16[256,128]{1,0:T(8,128)(2,1)S(1)}, bf16[256,128]{1,0:T(8,128)(2,1)S(1)}, u32[]{:S(2)}, u32[]{:S(2)}) collective-permute-start(bf16[256,128]{1,0:T(8,128)(2,1)S(1)} %get-tuple-element.31), channel_id=1, source_target_pairs={{0,4},{1,5},{2,6},{3,7},{4,0},{5,1},{6,2},{7,3},{8,12},{9,13},{10,... | collective-permute-start | bytes 196616 | tf_op jit(solution)/shard_map/ppermute | solution.py:334
  44.8 6.9 %collective-permute-start.24 = (bf16[256,128]{1,0:T(8,128)(2,1)S(1)}, bf16[256,128]{1,0:T(8,128)(2,1)S(1)}, u32[]{:S(2)}, u32[]{:S(2)}) collective-permute-start(bf16[256,128]{1,0:T(8,128)(2,1)S(1)} %get-tuple-element.32), channel_id=1, source_target_pairs={{0,6},{1,7},{2,4},{3,5},{4,2},{5,3},{6,0},{7,1},{8,14},{9,15},{10,... | collective-permute-start | bytes 196616 | tf_op jit(solution)/shard_map/ppermute | solution.py:334
  47.3 10.0 %collective-permute-start.25 = (bf16[256,128]{1,0:T(8,128)(2,1)S(1)}, bf16[256,128]{1,0:T(8,128)(2,1)S(1)}, u32[]{:S(2)}, u32[]{:S(2)}) collective-permute-start(bf16[256,128]{1,0:T(8,128)(2,1)S(1)} %add_terms.2.refs_0_.refs_4_), channel_id=1, source_target_pairs={{0,8},{8,0},{16,24},{24,16},{1,9},{9,1},{17,25},{25,17},{2,10},{10... | collective-permute-start | bytes 196616 | tf_op jit(solution)/shard_map/ppermute | solution.py:334
  50.6 7.4 %collective-permute-start.27 = (bf16[256,128]{1,0:T(8,128)(2,1)S(1)}, bf16[256,128]{1,0:T(8,128)(2,1)S(1)}, u32[]{:S(2)}, u32[]{:S(2)}) collective-permute-start(bf16[256,128]{1,0:T(8,128)(2,1)S(1)} %add_terms.2.refs_0_.refs_4_), channel_id=1, source_target_pairs={{0,16},{8,24},{16,0},{24,8},{1,17},{9,25},{17,1},{25,9},{2,18},{10... | collective-permute-start | bytes 196616 | tf_op jit(solution)/shard_map/ppermute | solution.py:334
  51.8 7.5 %collective-permute-start.28 = (bf16[256,128]{1,0:T(8,128)(2,1)S(1)}, bf16[256,128]{1,0:T(8,128)(2,1)S(1)}, u32[]{:S(2)}, u32[]{:S(2)}) collective-permute-start(bf16[256,128]{1,0:T(8,128)(2,1)S(1)} %add_terms.3.refs_5_), channel_id=1, source_target_pairs={{0,16},{8,24},{16,0},{24,8},{1,17},{9,25},{17,1},{25,9},{2,18},{10... | collective-permute-start | bytes 196616 | tf_op jit(solution)/shard_map/ppermute | solution.py:334
  54.5 6.1 %collective-permute-start.29 = (bf16[256,128]{1,0:T(8,128)(2,1)S(1)}, bf16[256,128]{1,0:T(8,128)(2,1)S(1)}, u32[]{:S(2)}, u32[]{:S(2)}) collective-permute-start(bf16[256,128]{1,0:T(8,128)(2,1)S(1)} %add_terms.2.refs_0_.refs_4_), channel_id=1, source_target_pairs={{8,16},{16,8},{9,17},{17,9},{10,18},{18,10},{11,19},{19,11},{12,20... | collective-permute-start | bytes 196616 | tf_op jit(solution)/shard_map/ppermute | solution.py:342
  55.2 5.4 %collective-permute-start.26 = (bf16[256,128]{1,0:T(8,128)(2,1)S(1)}, bf16[256,128]{1,0:T(8,128)(2,1)S(1)}, u32[]{:S(2)}, u32[]{:S(2)}) collective-permute-start(bf16[256,128]{1,0:T(8,128)(2,1)S(1)} %add_terms.3.refs_5_), channel_id=1, source_target_pairs={{0,8},{8,0},{16,24},{24,16},{1,9},{9,1},{17,25},{25,17},{2,10},{10... | collective-permute-start | bytes 196616 | tf_op jit(solution)/shard_map/ppermute | solution.py:334
  57.3 6.8 %collective-permute-start.31 = (bf16[256,128]{1,0:T(8,128)(2,1)S(1)}, bf16[256,128]{1,0:T(8,128)(2,1)S(1)}, u32[]{:S(2)}, u32[]{:S(2)}) collective-permute-start(bf16[256,128]{1,0:T(8,128)(2,1)S(1)} %add_terms.3.refs_5_), channel_id=1, source_target_pairs={{8,16},{16,8},{9,17},{17,9},{10,18},{18,10},{11,19},{19,11},{12,20... | collective-permute-start | bytes 196616 | tf_op jit(solution)/shard_map/ppermute | solution.py:342
  58.0 6.2 %collective-permute-start.30 = (bf16[256,128]{1,0:T(8,128)(2,1)S(1)}, bf16[256,128]{1,0:T(8,128)(2,1)S(1)}, u32[]{:S(2)}, u32[]{:S(2)}) collective-permute-start(bf16[256,128]{1,0:T(8,128)(2,1)S(1)} %collective-permute-done.27.refs_8_), channel_id=1, source_target_pairs={{16,24},{8,0},{17,25},{9,1},{18,26},{10,2},{19,27},{11,3},{20,28},... | collective-permute-start | bytes 196616 | tf_op jit(solution)/shard_map/ppermute | solution.py:343
  59.3 6.2 %collective-permute-start.32 = (bf16[256,128]{1,0:T(8,128)(2,1)S(1)}, bf16[256,128]{1,0:T(8,128)(2,1)S(1)}, u32[]{:S(2)}, u32[]{:S(2)}) collective-permute-start(bf16[256,128]{1,0:T(8,128)(2,1)S(1)} %collective-permute-done.28.refs_9_), channel_id=1, source_target_pairs={{16,24},{8,0},{17,25},{9,1},{18,26},{10,2},{19,27},{11,3},{20,28},... | collective-permute-start | bytes 196616 | tf_op jit(solution)/shard_map/ppermute | solution.py:343

commit v2 on v1

v2 whole, which is shorter than its diff:
```python
import functools

import jax
import jax.numpy as jnp
from jax import lax
from jax.experimental import pallas as pl
from jax.experimental.pallas import tpu as pltpu
from jax.sharding import PartitionSpec as P

D = 1024
DH = 128
EPS = 1e-05
GROUPS = 4
F32 = jnp.float32
BF16 = jnp.bfloat16
VMEM_BYTES = 12 * 1024 * 1024
CACHE_BYTES = 26 * 1024 * 1024
HALF_SCALE = 0.5 * DH ** (-0.5)

VM = pl.BlockSpec(memory_space=pltpu.VMEM)
SM = pl.BlockSpec(memory_space=pltpu.SMEM)
HB = pl.BlockSpec(memory_space=pltpu.HBM)
ANY = pl.BlockSpec(memory_space=pl.ANY)


def params(limit=VMEM_BYTES):
    return pltpu.CompilerParams(vmem_limit_bytes=limit)


def silu_of_half(half):
    return half * jnp.tanh(half) + half


SLOT, OFFSET, LIVE, COUNT = range(4)


def groups_of(chips):
    per = -(-(chips - 1) // (GROUPS - 1))
    return [[0]] + [list(range(at, min(at + per, chips))) for at in range(1, chips, per)]


def project_kernel(
    block_len, per, cand_hbm, gain_hbm, weight_hbm, user_hbm, block_hbm, len_hbm, *refs
):
    query_ref, gate_ref, plan, cand, gain, weight, user, block, length, sems, wsems = refs
    ints = [
        pltpu.make_async_copy(src, dst, sems.at[i])
        for i, (src, dst) in enumerate([(user_hbm, user), (block_hbm, block), (len_hbm, length)])
    ]
    rows_in = [
        pltpu.make_async_copy(src, dst, sems.at[3 + i])
        for i, (src, dst) in enumerate([(cand_hbm, cand), (gain_hbm, gain)])
    ]
    weights_in = [
        pltpu.make_async_copy(weight_hbm.at[i], weight.at[i], wsems.at[i]) for i in range(2)
    ]
    for copy in ints + rows_in + weights_in[::-1]:
        copy.start()
    me = lax.axis_index("cand")
    for copy in ints:
        copy.wait()
    for group in range(GROUPS):
        plan[group, COUNT, 0] = 0
    for s in range(user.shape[0]):
        owner, number = user[s], block[s]
        offset = owner ^ me
        group = (offset // 2 + per - 1) // per
        count = plan[group, COUNT, 0]
        live = jnp.where(number >= 0, length[owner] - number * block_len, 0)
        plan[group, SLOT, count] = s
        plan[group, OFFSET, count] = offset - jnp.where(group > 0, 2 * ((group - 1) * per + 1), 0)
        plan[GROUPS, LIVE, s] = live
        plan[group, COUNT, 0] = count + (number >= 0).astype(jnp.int32)

    for copy in rows_in:
        copy.wait()
    rows = cand[0].astype(F32)
    centred = rows - jnp.mean(rows, axis=-1, keepdims=True)
    var = jnp.mean(centred * centred, axis=-1, keepdims=True)
    normed = (centred * lax.rsqrt(var + EPS) * gain[...]).astype(BF16)
    weights_in[1].wait()
    half = 0.5 * jnp.dot(normed, weight[1], preferred_element_type=F32)
    query_ref[...] = (silu_of_half(half) * HALF_SCALE).astype(BF16)
    weights_in[0].wait()
    half = 0.5 * jnp.dot(normed, weight[0], preferred_element_type=F32)
    gate_ref[...] = silu_of_half(half).astype(BF16)


def project(
    candidates, input_gain, proj_weight, slot_user, slot_block, history_len, block_len, chips
):
    rows, cols = candidates.shape[1], proj_weight.shape[2]
    width = -(-(slot_user.shape[0] + 1) // 128) * 128
    per = -(-(chips - 1) // (GROUPS - 1))
    return pl.pallas_call(
        functools.partial(project_kernel, block_len, per),
        out_shape=[
            jax.ShapeDtypeStruct((rows, cols), BF16),
            jax.ShapeDtypeStruct((rows, cols), BF16),
            jax.ShapeDtypeStruct((GROUPS + 1, 4, width), jnp.int32),
        ],
        in_specs=[HB] * 6,
        out_specs=[VM, VM, SM],
        scratch_shapes=[
            pltpu.VMEM(candidates.shape, BF16),
            pltpu.VMEM((1, D), F32),
            pltpu.VMEM(proj_weight.shape, BF16),
            pltpu.SMEM(slot_user.shape, jnp.int32),
            pltpu.SMEM(slot_block.shape, jnp.int32),
            pltpu.SMEM(history_len.shape, jnp.int32),
            pltpu.SemaphoreType.DMA((5,)),
            pltpu.SemaphoreType.DMA((2,)),
        ],
        compiler_params=params(),
        cost_estimate=pl.CostEstimate(
            flops=4 * rows * cols * D, bytes_accessed=6 * cols * D, transcendentals=2 * rows * cols
        ),
        name="project",
    )(candidates, input_gain, proj_weight, slot_user, slot_block, history_len)


def load_kernel(plan, cache, kv, sems):
    slots, heads, block_len, _ = cache.shape

    def each_live(do):
        def visit(s, carry):
            @pl.when(plan[GROUPS, LIVE, s] > 0)
            def _():
                do(s)

            return carry

        lax.fori_loop(0, slots, visit, 0)

    def copy(s):
        return pltpu.make_async_copy(cache.at[s], kv.at[s], sems.at[s])

    def arrive(s):
        copy(s).wait()
        live = plan[GROUPS, LIVE, s]

        @pl.when(live < block_len)
        def _():
            event = lax.broadcasted_iota(jnp.int32, (block_len, DH), 0)
            for j in range(heads):
                vals = kv[s, j, :, DH:]
                kv[s, j, :, DH:] = jnp.where(event < live, vals, jnp.zeros_like(vals))

    each_live(lambda s: copy(s).start())
    each_live(arrive)


def load(plan, history_cache):
    return pl.pallas_call(
        load_kernel,
        out_shape=pltpu.VMEM(history_cache.shape, BF16),
        in_specs=[SM, HB],
        out_specs=VM,
        scratch_shapes=[pltpu.SemaphoreType.DMA((history_cache.shape[0],))],
        compiler_params=params(CACHE_BYTES),
        cost_estimate=pl.CostEstimate(
            flops=0, bytes_accessed=2 * history_cache.size, transcendentals=0
        ),
        name="load",
    )(plan, history_cache)


def attend_kernel(group, offsets, afters, plan, kv, *refs):
    queries, (near, far, query, total, wts) = refs[:offsets], refs[offsets + afters :]
    heads, block_len = kv.shape[1:3]
    half = block_len // 2
    tiles = [(j, e) for j in range(heads) for e in range(2)]
    count = plan[group, COUNT, 0]

    for d in range(offsets):
        query[d] = queries[d][...]
    total[...] = jnp.zeros_like(total)
    wts[...] = jnp.zeros_like(wts)

    def weigh(u, t):
        j, e = tiles[t]
        scores = lax.dot_general(
            query[plan[group, OFFSET, u], :, j * DH : (j + 1) * DH],
            kv[plan[group, SLOT, u], j, e * half : (e + 1) * half, :DH],
            (((1,), (1,)), ((), ())),
            preferred_element_type=F32,
        )
        wts[t] = silu_of_half(scores).astype(BF16)

    def gather(u, t):
        j, e = tiles[t]
        total[plan[group, OFFSET, u], :, j * DH : (j + 1) * DH] += jnp.dot(
            wts[t],
            kv[plan[group, SLOT, u], j, e * half : (e + 1) * half, DH:],
            preferred_element_type=F32,
        )

    last = len(tiles) - 1

    def step(u, carry):
        for t in range(len(tiles)):
            weigh(u, t)
            if t == 0:
                gather(jnp.maximum(u - 1, 0), last)
            else:
                gather(u, t - 1)
        return carry

    @pl.when(count > 0)
    def _():
        lax.fori_loop(0, count, step, 0)
        gather(count - 1, last)

    for d in range(offsets):
        if d % 2 == 0:
            near[d // 2] = total[d]
        else:
            far[d // 2] = total[d].astype(BF16)


def attend(queries, kv, plan, group, after):
    rows, cols = queries[0].shape
    slots, heads, block_len, width = kv.shape
    offsets = len(queries)
    work = slots * heads * rows * block_len // GROUPS
    return pl.pallas_call(
        functools.partial(attend_kernel, group, offsets, len(after)),
        out_shape=[
            jax.ShapeDtypeStruct((offsets // 2, rows, cols), F32),
            jax.ShapeDtypeStruct((offsets // 2, rows, cols), BF16),
        ],
        in_specs=[SM] + [VM] * (1 + offsets) + [ANY] * len(after),
        out_specs=[VM, VM],
        scratch_shapes=[
            pltpu.VMEM((offsets, rows, cols), BF16),
            pltpu.VMEM((offsets, rows, cols), F32),
            pltpu.VMEM((2 * heads, rows, block_len // 2), BF16),
        ],
        compiler_params=params(),
        cost_estimate=pl.CostEstimate(
            flops=2 * work * width, bytes_accessed=2 * work // rows * width, transcendentals=work
        ),
        name=f"attend_{group}",
    )(plan, kv, *queries, *after)


def pair_kernel(near, far, *refs):
    outs = refs[-near.shape[0] :]
    for e, out in enumerate(outs):
        out[...] = (near[e] + far[e].astype(F32)).astype(out.dtype)


def pair_terms(near, far, dtype, after):
    chips, rows, cols = near.shape
    return pl.pallas_call(
        pair_kernel,
        out_shape=[jax.ShapeDtypeStruct((rows, cols), dtype)] * chips,
        in_specs=[VM, VM] + [ANY] * len(after),
        out_specs=[VM] * chips,
        compiler_params=params(),
        name="pair_terms",
    )(near, far, *after)


def add_kernel(*refs):
    acc = refs[0][...]
    for ref in refs[1:-1]:
        acc = acc + ref[...].astype(F32)
    refs[-1][...] = acc.astype(BF16)


def add_terms(terms):
    return pl.pallas_call(
        add_kernel,
        out_shape=jax.ShapeDtypeStruct(terms[0].shape, BF16),
        in_specs=[VM] * len(terms),
        out_specs=VM,
        compiler_params=params(),
        name="add_terms",
    )(*terms)


def finish_kernel(shape, cand_ref, gain_ref, weight_ref, *refs):
    parts = len(shape)
    out_ref, refs = refs[-1], list(refs[:-1])
    gate = [refs.pop(0) for _ in range(parts)]
    blocks = [sum(refs.pop(0)[...].astype(F32) for _ in range(n)) for n in shape]
    me = lax.axis_index("hist")
    cols = out_ref.shape[2]
    mean = sum(jnp.sum(b, axis=-1, keepdims=True) for b in blocks) / D
    blocks = [b - mean for b in blocks]
    var = sum(jnp.sum(b * b, axis=-1, keepdims=True) for b in blocks) / D
    rstd = lax.rsqrt(var + EPS)
    acc = cand_ref[0, :, pl.ds(pl.multiple_of(me * cols, DH), cols)].astype(F32)
    for k in range(parts):
        at = pl.ds(pl.multiple_of((me ^ k) * cols, DH), cols)
        gained = blocks[k] * rstd * gain_ref[:, at]
        gated = (gained * gate[k][...].astype(F32)).astype(BF16)
        acc = acc + jnp.dot(gated, weight_ref[at, :], preferred_element_type=F32)
    out_ref[0] = acc.astype(BF16)


def finish(candidates, attention_gain, out_weight, gate, attn):
    rows, cols = gate[0].shape
    flat = [x for group in attn for x in group]
    return pl.pallas_call(
        functools.partial(finish_kernel, [len(group) for group in attn]),
        out_shape=jax.ShapeDtypeStruct((1, rows, cols), BF16),
        in_specs=[VM] * (3 + len(gate) + len(flat)),
        out_specs=VM,
        compiler_params=params(),
        name="finish",
    )(candidates, attention_gain.reshape(1, D), out_weight, *gate, *flat)


def swap(x, axis, bit):
    n = lax.axis_size(axis)
    return lax.ppermute(x, axis, [(i, i ^ bit) for i in range(n)])


def exchange(x, axis):
    n = lax.axis_size(axis)
    if n != 4:
        return [[x]] + [[swap(x, axis, k)] for k in range(1, n)]
    one, two = swap(x, axis, 1), swap(x, axis, 2)
    mid = lax.ppermute(x, axis, [(1, 2), (2, 1)])
    ends = lax.ppermute(two, axis, [(2, 3), (1, 0)])
    return [[x], [one], [two], [mid, ends]]


def local(
    candidates,
    input_gain,
    proj_weight,
    history_cache,
    slot_user,
    slot_block,
    history_len,
    attention_gain,
    out_weight,
):
    parts = lax.axis_size("hist")
    chips = lax.axis_size("cand") // 2
    in_hbm = functools.partial(pltpu.with_memory_space_constraint, memory_space=pltpu.HBM)
    query_own, gate_own, plan = project(
        in_hbm(candidates),
        in_hbm(input_gain.reshape(1, D)),
        in_hbm(proj_weight),
        in_hbm(slot_user),
        in_hbm(slot_block),
        in_hbm(history_len),
        history_cache.shape[2],
        chips,
    )
    query_near = [query_own] + [swap(query_own, "cand", 2 * e) for e in range(1, chips)]
    query_far = [swap(q, "cand", 1) for q in query_near]
    gate = [gate_own] + [swap(gate_own, "hist", k) for k in range(1, parts)]
    kv = load(plan, in_hbm(history_cache))
    groups = groups_of(chips)
    last = len(groups) - 1
    near, far, sent = [], [], []

    def send(g, after):
        pairs = pair_terms(near[g], far[g], BF16, after)
        sent.append([swap(pair, "cand", 2 * e) for e, pair in zip(groups[g], pairs)])
        return pairs

    for g, group in enumerate(groups):
        queries = [q for e in group for q in (query_near[e], query_far[e])]
        after = near[-1:]
        if g == last:
            after += gate[1:]
            if g > 2:
                after += send(1, [])[:1]
        terms = attend(queries, kv, plan, g, after)
        near.append(terms[0])
        far.append(swap(terms[1], "cand", 1))
    for g in range(1 + len(sent), last + 1):
        send(g, sent[0][:1] if g == last and g > 1 else [])
    terms = list(pair_terms(near[0], far[0], F32, near[1:2]))
    terms += [t for group in sent for t in group]
    attn = exchange(add_terms(terms), "hist")
    return finish(candidates, attention_gain, out_weight, gate, attn)


def solution(mesh):
    return jax.shard_map(
        local,
        mesh=mesh,
        in_specs=(
            P("cand", None, None),
            P(),
            P(None, None, "hist"),
            P("cand", "hist", None, None),
            P("cand"),
            P("cand"),
            P(),
            P(),
            P(None, "hist"),
        ),
        out_specs=P("cand", None, "hist"),
        check_vma=False,
    )
```

time: 67.2 us -> 71.3 us (1.061)
  starting transfers between devices: 34 us -> 19.4 us
  waiting for transfers between devices: 11.3 us -> 25.1 us
  Pallas kernels: 21.2 us -> 26.8 us
    ppermute x29 -> x19, waiting for transfers between devices: 6.5 us -> 19.5 us  [swap(): return lax.ppermute(x, axis, [(i, i ^ bit) for i in range(n)])]
    ppermute x29 -> x19, starting transfers between devices: 30.1 us -> 17.5 us  [swap(): return lax.ppermute(x, axis, [(i, i ^ bit) for i in range(n)])]
    pallas_call x7 -> x11, Pallas kernels: 21.1 us -> 26.8 us  [the longest x4 16.6 us: attend(): pl.pallas_call(functools.partial(attend_kernel, group, offsets, len(after...]
    ppermute x2 -> x1, starting transfers between devices: 2.58 us -> 1.28 us  [exchange(): ends = lax.ppermute(two, axis, [(2, 3), (1, 0)])]
    ppermute x2 -> x1, waiting for transfers between devices: 4.84 us -> 5.54 us  [exchange(): ends = lax.ppermute(two, axis, [(2, 3), (1, 0)])]
  transfers between devices with their start and end apart: 33 -> 21, of which waited for: 6 -> 7; matrix products, arithmetic and copies ran while one was open for 0% -> 0% of each run, Pallas kernels for 25% -> 32%
where the time goes in v2:
time: 71.3 us; the launch traced here: 71.5 us
  Pallas kernels  26.8 us (38%)
  waiting for transfers between devices  25.1 us (35%)
  starting transfers between devices  19.4 us (27%)
    ppermute x19, waiting for transfers between devices, swap(): return lax.ppermute(x, axis, [(i, i ^ bit) for i in range(n)])  19.5 us
    ppermute x19, starting transfers between devices, swap(): return lax.ppermute(x, axis, [(i, i ^ bit) for i in range(n)])  17.5 us
    pallas_call x4, Pallas kernels, attend(): pl.pallas_call(functools.partial(attend_kernel, group, offsets, len(after...  16.6 us
    pallas_call x1, Pallas kernels, load(): pl.pallas_call(load_kernel, out_shape=pltpu.VMEM(history_cache.shape, BF1...  6.01 us
    ppermute x1, waiting for transfers between devices, exchange(): ends = lax.ppermute(two, axis, [(2, 3), (1, 0)])  5.54 us
    pallas_call x1, Pallas kernels, project(): pl.pallas_call(functools.partial(project_kernel, block_len, per), out_sha...  2.79 us
  transfers between devices with their start and end apart: 21, of which 7 were waited for; matrix products, arithmetic and copies ran while one was open for 0% of the time, Pallas kernels for 32%

profile of v2, /device:TPU:0, one launch (start us, length us, event | category | flops | bytes accessed | tf_op | source)
XLA Modules:
  0.0 71.5 jit_solution(8023505583329317963)
XLA Ops:
  0.0 2.8 %project.1 = (bf16[256,256]{1,0:T(8,128)(2,1)S(1)}, bf16[256,256]{1,0:T(8,128)(2,1)S(1)}, s32[5,4,128]{2,1,0:T(4,128)S(1)}) custom-call(bf16[1,256,1024]{2,1,0:T(8,128)(2,1)} %cand_ref.1, f32[1,1024]{1,0:T(1,128)} %bitcast.3, bf16[2,1024,256]{2,1,0:T(8,128)(2,1)} %weight_hbm.1, s32[40]{0:T(128)} %user_hbm.1, s32[40]{0:T(128)} %block_hbm.1, s32[8]{0:T(128)} %len_hbm.1), custom_call_target="tpu_custom_call" | custom-call | flops 268435456 | bytes 1572864 | tf_op jit(solution)/shard_map/project/pallas_call | solution.py:95
  2.8 3.0 %collective-permute-start.5 = (bf16[256,256]{1,0:T(8,128)(2,1)S(1)}, bf16[256,256]{1,0:T(8,128)(2,1)S(1)}, u32[]{:S(2)}, u32[]{:S(2)}) collective-permute-start(bf16[256,256]{1,0:T(8,128)(2,1)S(1)} %get-tuple-element.18.refs_0_), channel_id=1, source_target_pairs={{0,2},{1,3},{2,0},{3,1},{4,6},{5,7},{6,4},{7,5},{8,10},{9,11},{10,... | collective-permute-start | bytes 393224 | tf_op jit(solution)/shard_map/ppermute | solution.py:318
  5.8 1.5 %collective-permute-start.9 = (bf16[256,256]{1,0:T(8,128)(2,1)S(1)}, bf16[256,256]{1,0:T(8,128)(2,1)S(1)}, u32[]{:S(2)}, u32[]{:S(2)}) collective-permute-start(bf16[256,256]{1,0:T(8,128)(2,1)S(1)} %get-tuple-element.18.refs_0_), channel_id=1, source_target_pairs={{0,4},{1,5},{2,6},{3,7},{4,0},{5,1},{6,2},{7,3},{8,12},{9,13},{10,... | collective-permute-start | bytes 393224 | tf_op jit(solution)/shard_map/ppermute | solution.py:318
  7.3 0.0 collective-permute-start.3
  7.3 2.0 %collective-permute-done.5.refs_0_ = bf16[256,256]{1,0:T(8,128)(2,1)S(1)} collective-permute-done((bf16[256,256]{1,0:T(8,128)(2,1)S(1)}, bf16[256,256]{1,0:T(8,128)(2,1)S(1)}, u32[]{:S(2)}, u32[]{:S(2)}) %collective-permute-start.5) | collective-permute-done | bytes 131104 | tf_op jit(solution)/shard_map/ppermute | solution.py:318
  9.3 0.0 collective-permute-start.6
  9.3 2.7 %collective-permute-start.13 = (bf16[256,256]{1,0:T(8,128)(2,1)S(1)}, bf16[256,256]{1,0:T(8,128)(2,1)S(1)}, u32[]{:S(2)}, u32[]{:S(2)}) collective-permute-start(bf16[256,256]{1,0:T(8,128)(2,1)S(1)} %get-tuple-element.18.refs_0_), channel_id=1, source_target_pairs={{0,6},{1,7},{2,4},{3,5},{4,2},{5,3},{6,0},{7,1},{8,14},{9,15},{10,... | collective-permute-start | bytes 393224 | tf_op jit(solution)/shard_map/ppermute | solution.py:318
  12.0 6.0 %load.1.kv = bf16[40,2,512,256]{3,2,1,0:T(8,128)(2,1)S(1)} custom-call(s32[5,4,128]{2,1,0:T(4,128)S(1)} %get-tuple-element.17.plan, bf16[40,2,512,256]{3,2,1,0:T(8,128)(2,1)} %cache.1), custom_call_target="tpu_custom_call" | custom-call | bytes 20971520 | tf_op jit(solution)/shard_map/load/pallas_call | solution.py:154
  18.0 0.0 collective-permute-done.9.refs_0_
  18.0 0.4 collective-permute-start.10
  18.5 0.0 collective-permute-done.3.refs_1_
  18.5 4.4 %attend_0.1 = (f32[1,256,256]{2,1,0:T(8,128)S(1)}, bf16[1,256,256]{2,1,0:T(8,128)(2,1)S(1)}) custom-call(s32[5,4,128]{2,1,0:T(4,128)S(1)} %get-tuple-element.17.plan, bf16[40,2,512,256]{3,2,1,0:T(8,128)(2,1)S(1)} %load.1.kv, bf16[256,256]{1,0:T(8,128)(2,1)S(1)} %get-tuple-element.18.refs_0_, bf16[256,256]{1,0:T(8,128)(2,1)S(1)} %collective-permute-done.3.refs_1_), custom_call_target="tpu_custom_call" | custom-call | flops 1342177280 | bytes 5242880 | tf_op jit(solution)/shard_map/attend_0/pallas_call | solution.py:226
  22.9 0.0 collective-permute-done.6.refs_1_
  22.9 2.4 %attend_1.1 = (f32[1,256,256]{2,1,0:T(8,128)S(1)}, bf16[1,256,256]{2,1,0:T(8,128)(2,1)S(1)}) custom-call(s32[5,4,128]{2,1,0:T(4,128)S(1)} %get-tuple-element.17.plan, bf16[40,2,512,256]{3,2,1,0:T(8,128)(2,1)S(1)} %load.1.kv, bf16[256,256]{1,0:T(8,128)(2,1)S(1)} %collective-permute-done.5.refs_0_, bf16[256,256]{1,0:T(8,128)(2,1)S(1)} %collective-permute-done.6.refs_1_, ...), custom_call_target="tpu_custom_call" | custom-call | flops 1342177280 | bytes 5242880 | tf_op jit(solution)/shard_map/attend_1/pallas_call | solution.py:226
  25.3 0.7 collective-permute-start.7
  26.0 1.6 %collective-permute-start = (bf16[256,256]{1,0:T(8,128)(2,1)S(1)}, bf16[256,256]{1,0:T(8,128)(2,1)S(1)}, u32[]{:S(2)}, u32[]{:S(2)}) collective-permute-start(bf16[256,256]{1,0:T(8,128)(2,1)S(1)} %get-tuple-element.16.refs_0_), channel_id=1, source_target_pairs={{0,8},{8,0},{16,24},{24,16},{1,9},{9,1},{17,25},{25,17},{2,10},{10... | collective-permute-start | bytes 393224 | tf_op jit(solution)/shard_map/ppermute | solution.py:318
  27.6 2.6 %collective-permute-start.1 = (bf16[256,256]{1,0:T(8,128)(2,1)S(1)}, bf16[256,256]{1,0:T(8,128)(2,1)S(1)}, u32[]{:S(2)}, u32[]{:S(2)}) collective-permute-start(bf16[256,256]{1,0:T(8,128)(2,1)S(1)} %get-tuple-element.16.refs_0_), channel_id=1, source_target_pairs={{0,16},{8,24},{16,0},{24,8},{1,17},{9,25},{17,1},{25,9},{2,18},{10... | collective-permute-start | bytes 393224 | tf_op jit(solution)/shard_map/ppermute | solution.py:318
  30.2 0.0 collective-permute-done.13.refs_0_
  30.2 0.2 collective-permute-start.2
  30.4 0.0 collective-permute-done.10.refs_1_
  30.4 0.0 collective-permute-start.14
  30.4 0.0 copy-start
  30.4 0.0 copy-start.1
  30.4 0.0 copy-start.2
  30.4 5.4 %attend_2.1 = (f32[1,256,256]{2,1,0:T(8,128)S(1)}, bf16[1,256,256]{2,1,0:T(8,128)(2,1)S(1)}) custom-call(s32[5,4,128]{2,1,0:T(4,128)S(1)} %get-tuple-element.17.plan, bf16[40,2,512,256]{3,2,1,0:T(8,128)(2,1)S(1)} %load.1.kv, bf16[256,256]{1,0:T(8,128)(2,1)S(1)} %collective-permute-done.9.refs_0_, bf16[256,256]{1,0:T(8,128)(2,1)S(1)} %collective-permute-done.10.refs_1_, ...), custom_call_target="tpu_custom_call" | custom-call | flops 1342177280 | bytes 5242880 | tf_op jit(solution)/shard_map/attend_2/pallas_call | solution.py:226
  35.8 0.0 collective-permute-done.7.far
  35.8 0.1 collective-permute-start.11
  35.9 0.0 collective-permute-done.refs_3_.refs_1_
  35.9 0.1 collective-permute-start.8
  36.0 4.5 %collective-permute-done.1.refs_4_.refs_2_ = bf16[256,256]{1,0:T(8,128)(2,1)S(1)} collective-permute-done((bf16[256,256]{1,0:T(8,128)(2,1)S(1)}, bf16[256,256]{1,0:T(8,128)(2,1)S(1)}, u32[]{:S(2)}, u32[]{:S(2)}) %collective-permute-start.1) | collective-permute-done | bytes 131104 | tf_op jit(solution)/shard_map/ppermute | solution.py:318
  40.5 0.0 collective-permute-done.2.refs_5_.refs_3_
  40.5 0.0 collective-permute-done.14.refs_1_
  40.5 4.4 %attend_3.1 = (f32[1,256,256]{2,1,0:T(8,128)S(1)}, bf16[1,256,256]{2,1,0:T(8,128)(2,1)S(1)}) custom-call(s32[5,4,128]{2,1,0:T(4,128)S(1)} %get-tuple-element.17.plan, bf16[40,2,512,256]{3,2,1,0:T(8,128)(2,1)S(1)} %load.1.kv, bf16[256,256]{1,0:T(8,128)(2,1)S(1)} %collective-permute-done.13.refs_0_, bf16[256,256]{1,0:T(8,128)(2,1)S(1)} %collective-permute-done.14.refs_1_, ...), custom_call_target="tpu_custom_call" | custom-call | flops 1342177280 | bytes 5242880 | tf_op jit(solution)/shard_map/attend_3/pallas_call | solution.py:226
  44.9 0.1 collective-permute-start.15
  45.0 0.5 collective-permute-start.4
  45.5 0.0 collective-permute-done.11.far
  45.5 0.7 collective-permute-start.12
  46.2 0.0 collective-permute-done.8.refs_0_.refs_1_
  46.2 0.1 collective-permute-done.15.far
  46.3 0.1 collective-permute-start.16
  46.4 0.1 collective-permute-done.4.far
  46.5 7.3 %collective-permute-done.12.refs_2_ = bf16[256,256]{1,0:T(8,128)(2,1)S(1)} collective-permute-done((bf16[256,256]{1,0:T(8,128)(2,1)S(1)}, bf16[256,256]{1,0:T(8,128)(2,1)S(1)}, u32[]{:S(2)}, u32[]{:S(2)}) %collective-permute-start.12) | collective-permute-done | bytes 131104 | tf_op jit(solution)/shard_map/ppermute | solution.py:318
  53.9 0.0 collective-permute-done.16.refs_3_
  53.9 0.1 add_terms.1.refs_4_
  53.9 3.3 %collective-permute-start.18 = (bf16[256,256]{1,0:T(8,128)(2,1)S(1)}, bf16[256,256]{1,0:T(8,128)(2,1)S(1)}, u32[]{:S(2)}, u32[]{:S(2)}) collective-permute-start(bf16[256,256]{1,0:T(8,128)(2,1)S(1)} %add_terms.1.refs_4_), channel_id=1, source_target_pairs={{0,16},{8,24},{16,0},{24,8},{1,17},{9,25},{17,1},{25,9},{2,18},{10... | collective-permute-start | bytes 393224 | tf_op jit(solution)/shard_map/ppermute | solution.py:318
  57.2 0.0 collective-permute-start.17
  57.2 0.7 collective-permute-start.19
  57.9 5.5 %collective-permute-done.18.refs_6_ = bf16[256,256]{1,0:T(8,128)(2,1)S(1)} collective-permute-done((bf16[256,256]{1,0:T(8,128)(2,1)S(1)}, bf16[256,256]{1,0:T(8,128)(2,1)S(1)}, u32[]{:S(2)}, u32[]{:S(2)}) %collective-permute-start.18) | collective-permute-done | bytes 131104 | tf_op jit(solution)/shard_map/ppermute | solution.py:318
  63.4 1.3 %collective-permute-start.20 = (bf16[256,256]{1,0:T(8,128)(2,1)S(1)}, bf16[256,256]{1,0:T(8,128)(2,1)S(1)}, u32[]{:S(2)}, u32[]{:S(2)}) collective-permute-start(bf16[256,256]{1,0:T(8,128)(2,1)S(1)} %collective-permute-done.18.refs_6_), channel_id=1, source_target_pairs={{16,24},{8,0},{17,25},{9,1},{18,26},{10,2},{19,27},{11,3},{20,28},... | collective-permute-start | bytes 393224 | tf_op jit(solution)/shard_map/ppermute | solution.py:327
  64.7 0.0 collective-permute-done.17.refs_5_
  64.7 0.0 collective-permute-done.19.refs_7_
  64.7 5.5 %collective-permute-done.20.refs_8_ = bf16[256,256]{1,0:T(8,128)(2,1)S(1)} collective-permute-done((bf16[256,256]{1,0:T(8,128)(2,1)S(1)}, bf16[256,256]{1,0:T(8,128)(2,1)S(1)}, u32[]{:S(2)}, u32[]{:S(2)}) %collective-permute-start.20) | collective-permute-done | bytes 131104 | tf_op jit(solution)/shard_map/ppermute | solution.py:327
  70.2 0.0 copy-done
  70.2 0.0 copy-done.1
  70.2 0.0 copy-done.2
  70.2 1.3 %finish.1 = bf16[1,256,256]{2,1,0:T(8,128)(2,1)} custom-call(bf16[1,256,1024]{2,1,0:T(8,128)(2,1)S(1)} %copy-done, f32[1,1024]{1,0:T(1,128)S(1)} %bitcast.2, bf16[1024,256]{1,0:T(8,128)(2,1)S(1)} %copy-done.1, bf16[256,256]{1,0:T(8,128)(2,1)S(1)} %get-tuple-element.16.refs_0_, bf16[256,256]{1,0:T(8,128)(2,1)S(1)} %collective-permute-done.refs_3_.refs_1_, ...), custom_call_target="tpu_custom_call" | custom-call | tf_op jit(solution)/shard_map/finish/pallas_call | solution.py:306
  (4 shorter events, 0.1 us)
Async XLA Ops:
  2.8 6.5 %collective-permute-start.5 = (bf16[256,256]{1,0:T(8,128)(2,1)S(1)}, bf16[256,256]{1,0:T(8,128)(2,1)S(1)}, u32[]{:S(2)}, u32[]{:S(2)}) collective-permute-start(bf16[256,256]{1,0:T(8,128)(2,1)S(1)} %get-tuple-element.18.refs_0_), channel_id=1, source_target_pairs={{0,2},{1,3},{2,0},{3,1},{4,6},{5,7},{6,4},{7,5},{8,10},{9,11},{10,... | collective-permute-start | bytes 393224 | tf_op jit(solution)/shard_map/ppermute | solution.py:318
  5.8 12.2 %collective-permute-start.9 = (bf16[256,256]{1,0:T(8,128)(2,1)S(1)}, bf16[256,256]{1,0:T(8,128)(2,1)S(1)}, u32[]{:S(2)}, u32[]{:S(2)}) collective-permute-start(bf16[256,256]{1,0:T(8,128)(2,1)S(1)} %get-tuple-element.18.refs_0_), channel_id=1, source_target_pairs={{0,4},{1,5},{2,6},{3,7},{4,0},{5,1},{6,2},{7,3},{8,12},{9,13},{10,... | collective-permute-start | bytes 393224 | tf_op jit(solution)/shard_map/ppermute | solution.py:318
  7.3 11.1 %collective-permute-start.3 = (bf16[256,256]{1,0:T(8,128)(2,1)S(1)}, bf16[256,256]{1,0:T(8,128)(2,1)S(1)}, u32[]{:S(2)}, u32[]{:S(2)}) collective-permute-start(bf16[256,256]{1,0:T(8,128)(2,1)S(1)} %get-tuple-element.18.refs_0_), channel_id=1, source_target_pairs={{0,1},{1,0},{2,3},{3,2},{4,5},{5,4},{6,7},{7,6},{8,9},{9,8},{10,11... | collective-permute-start | bytes 393224 | tf_op jit(solution)/shard_map/ppermute | solution.py:318
  9.3 13.6 %collective-permute-start.6 = (bf16[256,256]{1,0:T(8,128)(2,1)S(1)}, bf16[256,256]{1,0:T(8,128)(2,1)S(1)}, u32[]{:S(2)}, u32[]{:S(2)}) collective-permute-start(bf16[256,256]{1,0:T(8,128)(2,1)S(1)} %collective-permute-done.5.refs_0_), channel_id=1, source_target_pairs={{0,1},{1,0},{2,3},{3,2},{4,5},{5,4},{6,7},{7,6},{8,9},{9,8},{10,11... | collective-permute-start | bytes 393224 | tf_op jit(solution)/shard_map/ppermute | solution.py:318
  9.3 20.9 %collective-permute-start.13 = (bf16[256,256]{1,0:T(8,128)(2,1)S(1)}, bf16[256,256]{1,0:T(8,128)(2,1)S(1)}, u32[]{:S(2)}, u32[]{:S(2)}) collective-permute-start(bf16[256,256]{1,0:T(8,128)(2,1)S(1)} %get-tuple-element.18.refs_0_), channel_id=1, source_target_pairs={{0,6},{1,7},{2,4},{3,5},{4,2},{5,3},{6,0},{7,1},{8,14},{9,15},{10,... | collective-permute-start | bytes 393224 | tf_op jit(solution)/shard_map/ppermute | solution.py:318
  18.0 12.4 %collective-permute-start.10 = (bf16[256,256]{1,0:T(8,128)(2,1)S(1)}, bf16[256,256]{1,0:T(8,128)(2,1)S(1)}, u32[]{:S(2)}, u32[]{:S(2)}) collective-permute-start(bf16[256,256]{1,0:T(8,128)(2,1)S(1)} %collective-permute-done.9.refs_0_), channel_id=1, source_target_pairs={{0,1},{1,0},{2,3},{3,2},{4,5},{5,4},{6,7},{7,6},{8,9},{9,8},{10,11... | collective-permute-start | bytes 393224 | tf_op jit(solution)/shard_map/ppermute | solution.py:318
  25.3 10.5 %collective-permute-start.7 = (bf16[1,256,256]{2,1,0:T(8,128)(2,1)S(1)}, bf16[1,256,256]{2,1,0:T(8,128)(2,1)S(1)}, u32[]{:S(2)}, u32[]{:S(2)}) collective-permute-start(bf16[1,256,256]{2,1,0:T(8,128)(2,1)S(1)} %get-tuple-element.22), channel_id=1, source_target_pairs={{0,1},{1,0},{2,3},{3,2},{4,5},{5,4},{6,7},{7,6},{8,9},{9,8},{10,11... | collective-permute-start | bytes 393224 | tf_op jit(solution)/shard_map/ppermute | solution.py:318
  26.0 9.9 %collective-permute-start = (bf16[256,256]{1,0:T(8,128)(2,1)S(1)}, bf16[256,256]{1,0:T(8,128)(2,1)S(1)}, u32[]{:S(2)}, u32[]{:S(2)}) collective-permute-start(bf16[256,256]{1,0:T(8,128)(2,1)S(1)} %get-tuple-element.16.refs_0_), channel_id=1, source_target_pairs={{0,8},{8,0},{16,24},{24,16},{1,9},{9,1},{17,25},{25,17},{2,10},{10... | collective-permute-start | bytes 393224 | tf_op jit(solution)/shard_map/ppermute | solution.py:318
  27.6 12.9 %collective-permute-start.1 = (bf16[256,256]{1,0:T(8,128)(2,1)S(1)}, bf16[256,256]{1,0:T(8,128)(2,1)S(1)}, u32[]{:S(2)}, u32[]{:S(2)}) collective-permute-start(bf16[256,256]{1,0:T(8,128)(2,1)S(1)} %get-tuple-element.16.refs_0_), channel_id=1, source_target_pairs={{0,16},{8,24},{16,0},{24,8},{1,17},{9,25},{17,1},{25,9},{2,18},{10... | collective-permute-start | bytes 393224 | tf_op jit(solution)/shard_map/ppermute | solution.py:318
  30.2 10.3 %collective-permute-start.2 = (bf16[256,256]{1,0:T(8,128)(2,1)S(1)}, bf16[256,256]{1,0:T(8,128)(2,1)S(1)}, u32[]{:S(2)}, u32[]{:S(2)}) collective-permute-start(bf16[256,256]{1,0:T(8,128)(2,1)S(1)} %get-tuple-element.16.refs_0_), channel_id=1, source_target_pairs={{0,24},{8,16},{16,8},{24,0},{1,25},{9,17},{17,9},{25,1},{2,26},{10... | collective-permute-start | bytes 393224 | tf_op jit(solution)/shard_map/ppermute | solution.py:318
  30.4 10.1 %collective-permute-start.14 = (bf16[256,256]{1,0:T(8,128)(2,1)S(1)}, bf16[256,256]{1,0:T(8,128)(2,1)S(1)}, u32[]{:S(2)}, u32[]{:S(2)}) collective-permute-start(bf16[256,256]{1,0:T(8,128)(2,1)S(1)} %collective-permute-done.13.refs_0_), channel_id=1, source_target_pairs={{0,1},{1,0},{2,3},{3,2},{4,5},{5,4},{6,7},{7,6},{8,9},{9,8},{10,11... | collective-permute-start | bytes 393224 | tf_op jit(solution)/shard_map/ppermute | solution.py:318
  30.4 39.8 %copy-start = (bf16[1,256,1024]{2,1,0:T(8,128)(2,1)S(1)}, bf16[1,256,1024]{2,1,0:T(8,128)(2,1)}, u32[]{:S(2)}) copy-start(bf16[1,256,1024]{2,1,0:T(8,128)(2,1)} %cand_ref.1) | copy-start | bytes 1572868
  30.4 39.8 %copy-start.1 = (bf16[1024,256]{1,0:T(8,128)(2,1)S(1)}, bf16[1024,256]{1,0:T(8,128)(2,1)}, u32[]{:S(2)}) copy-start(bf16[1024,256]{1,0:T(8,128)(2,1)} %weight_ref.1) | copy-start | bytes 1572868
  30.4 39.8 %copy-start.2 = (f32[1024]{0:T(1024)S(1)}, f32[1024]{0:T(1024)}, u32[]{:S(2)}) copy-start(f32[1024]{0:T(1024)} %param.16) | copy-start | bytes 12292
  35.8 9.7 %collective-permute-start.11 = (bf16[1,256,256]{2,1,0:T(8,128)(2,1)S(1)}, bf16[1,256,256]{2,1,0:T(8,128)(2,1)S(1)}, u32[]{:S(2)}, u32[]{:S(2)}) collective-permute-start(bf16[1,256,256]{2,1,0:T(8,128)(2,1)S(1)} %get-tuple-element.24), channel_id=1, source_target_pairs={{0,1},{1,0},{2,3},{3,2},{4,5},{5,4},{6,7},{7,6},{8,9},{9,8},{10,11... | collective-permute-start | bytes 393224 | tf_op jit(solution)/shard_map/ppermute | solution.py:318
  35.9 10.2 %collective-permute-start.8 = (bf16[256,256]{1,0:T(8,128)(2,1)S(1)}, bf16[256,256]{1,0:T(8,128)(2,1)S(1)}, u32[]{:S(2)}, u32[]{:S(2)}) collective-permute-start(bf16[256,256]{1,0:T(8,128)(2,1)S(1)} %pair_terms.5.refs_6_), channel_id=1, source_target_pairs={{0,2},{1,3},{2,0},{3,1},{4,6},{5,7},{6,4},{7,5},{8,10},{9,11},{10,... | collective-permute-start | bytes 393224 | tf_op jit(solution)/shard_map/ppermute | solution.py:318
  44.9 1.4 %collective-permute-start.15 = (bf16[1,256,256]{2,1,0:T(8,128)(2,1)S(1)}, bf16[1,256,256]{2,1,0:T(8,128)(2,1)S(1)}, u32[]{:S(2)}, u32[]{:S(2)}) collective-permute-start(bf16[1,256,256]{2,1,0:T(8,128)(2,1)S(1)} %get-tuple-element.26), channel_id=1, source_target_pairs={{0,1},{1,0},{2,3},{3,2},{4,5},{5,4},{6,7},{7,6},{8,9},{9,8},{10,11... | collective-permute-start | bytes 393224 | tf_op jit(solution)/shard_map/ppermute | solution.py:318
  45.0 1.5 %collective-permute-start.4 = (bf16[1,256,256]{2,1,0:T(8,128)(2,1)S(1)}, bf16[1,256,256]{2,1,0:T(8,128)(2,1)S(1)}, u32[]{:S(2)}, u32[]{:S(2)}) collective-permute-start(bf16[1,256,256]{2,1,0:T(8,128)(2,1)S(1)} %get-tuple-element.20), channel_id=1, source_target_pairs={{0,1},{1,0},{2,3},{3,2},{4,5},{5,4},{6,7},{7,6},{8,9},{9,8},{10,11... | collective-permute-start | bytes 393224 | tf_op jit(solution)/shard_map/ppermute | solution.py:318
  45.5 8.4 %collective-permute-start.12 = (bf16[256,256]{1,0:T(8,128)(2,1)S(1)}, bf16[256,256]{1,0:T(8,128)(2,1)S(1)}, u32[]{:S(2)}, u32[]{:S(2)}) collective-permute-start(bf16[256,256]{1,0:T(8,128)(2,1)S(1)} %pair_terms.6), channel_id=1, source_target_pairs={{0,4},{1,5},{2,6},{3,7},{4,0},{5,1},{6,2},{7,3},{8,12},{9,13},{10,... | collective-permute-start | bytes 393224 | tf_op jit(solution)/shard_map/ppermute | solution.py:318
  46.3 7.5 %collective-permute-start.16 = (bf16[256,256]{1,0:T(8,128)(2,1)S(1)}, bf16[256,256]{1,0:T(8,128)(2,1)S(1)}, u32[]{:S(2)}, u32[]{:S(2)}) collective-permute-start(bf16[256,256]{1,0:T(8,128)(2,1)S(1)} %pair_terms.7), channel_id=1, source_target_pairs={{0,6},{1,7},{2,4},{3,5},{4,2},{5,3},{6,0},{7,1},{8,14},{9,15},{10,... | collective-permute-start | bytes 393224 | tf_op jit(solution)/shard_map/ppermute | solution.py:318
  53.9 9.5 %collective-permute-start.18 = (bf16[256,256]{1,0:T(8,128)(2,1)S(1)}, bf16[256,256]{1,0:T(8,128)(2,1)S(1)}, u32[]{:S(2)}, u32[]{:S(2)}) collective-permute-start(bf16[256,256]{1,0:T(8,128)(2,1)S(1)} %add_terms.1.refs_4_), channel_id=1, source_target_pairs={{0,16},{8,24},{16,0},{24,8},{1,17},{9,25},{17,1},{25,9},{2,18},{10... | collective-permute-start | bytes 393224 | tf_op jit(solution)/shard_map/ppermute | solution.py:318
  57.2 7.4 %collective-permute-start.17 = (bf16[256,256]{1,0:T(8,128)(2,1)S(1)}, bf16[256,256]{1,0:T(8,128)(2,1)S(1)}, u32[]{:S(2)}, u32[]{:S(2)}) collective-permute-start(bf16[256,256]{1,0:T(8,128)(2,1)S(1)} %add_terms.1.refs_4_), channel_id=1, source_target_pairs={{0,8},{8,0},{16,24},{24,16},{1,9},{9,1},{17,25},{25,17},{2,10},{10... | collective-permute-start | bytes 393224 | tf_op jit(solution)/shard_map/ppermute | solution.py:318
  57.2 7.5 %collective-permute-start.19 = (bf16[256,256]{1,0:T(8,128)(2,1)S(1)}, bf16[256,256]{1,0:T(8,128)(2,1)S(1)}, u32[]{:S(2)}, u32[]{:S(2)}) collective-permute-start(bf16[256,256]{1,0:T(8,128)(2,1)S(1)} %add_terms.1.refs_4_), channel_id=1, source_target_pairs={{8,16},{16,8},{9,17},{17,9},{10,18},{18,10},{11,19},{19,11},{12,20... | collective-permute-start | bytes 393224 | tf_op jit(solution)/shard_map/ppermute | solution.py:326
  63.4 6.8 %collective-permute-start.20 = (bf16[256,256]{1,0:T(8,128)(2,1)S(1)}, bf16[256,256]{1,0:T(8,128)(2,1)S(1)}, u32[]{:S(2)}, u32[]{:S(2)}) collective-permute-start(bf16[256,256]{1,0:T(8,128)(2,1)S(1)} %collective-permute-done.18.refs_6_), channel_id=1, source_target_pairs={{16,24},{8,0},{17,25},{9,1},{18,26},{10,2},{19,27},{11,3},{20,28},... | collective-permute-start | bytes 393224 | tf_op jit(solution)/shard_map/ppermute | solution.py:327
